TPU v7x, 512 devices: a whole 4x8x8 slice. The times are simulated.
512 devices in a mesh: rows: 32 (over x, z), vecs: 16 (over y, core).
Axes of the slice: x: 4, y: 8, z: 8, core: 2. Of those that a mesh axis runs over, the one named last changes fastest.
Arguments:
- tiles: bfloat16 [128, 6, 128, 128], P('rows'), as said below
- columns: int32 [128, 6], P('rows'), may hold values from 0 to 127, as said below
- start_vectors: float32 [1024, 16384], P('vecs', 'rows'), may hold values from -6 to 6
Outputs:
- basis: float32 [1024, 16384], P('vecs', 'rows')
Inputs may be any that keep to these rules, and one draw needn't show every extreme that they name: `columns`: the 6 column blocks of row block b are distinct; they are b, b - 1, b + 1 and three of b - 3, b - 2, b + 2, b + 3, all modulo 128, the first three in this order. The pattern is symmetric: block c is among those of row block b exactly when b is among those of row block c. `tiles`: H is symmetric: the tile of row block b at column block c is the transpose of the tile of row block c at column block b.
All inputs are finite; a program needn't handle non-finite values.
Results may differ from a plain program's by a relative error of at most 0.0003.
Values sent between devices are 32-bit elements; how exact they have to be, the bound alone decides.
A program may use at most 64 MiB of HBM per device.

v0:
```python
import jax
import jax.numpy as jnp
from jax import lax
from jax.sharding import PartitionSpec as P

BS = 128
HB = 3
STEPS = 4


def with_halo(shard, sides, width):
    for axis, dim in sides:
        devices, length = (lax.axis_size(axis), shard.shape[dim])
        up = [(i, (i + 1) % devices) for i in range(devices)]
        down = [(j, i) for i, j in up]
        last = lax.slice_in_dim(shard, length - width, length, axis=dim)
        initial = lax.slice_in_dim(shard, 0, width, axis=dim)
        before = lax.ppermute(last, axis, up)
        after = lax.ppermute(initial, axis, down)
        shard = jnp.concatenate([before, shard, after], axis=dim)
    return shard


def operate(field, tiles32, slots):
    extended = with_halo(field, (("rows", 1),), HB * BS)
    width = field.shape[0]
    blocks_here = tiles32.shape[0]
    blocked = extended.reshape(width, blocks_here + 2 * HB, BS)
    picked = blocked[:, slots]
    result = jnp.einsum("mbtj,btij->mbi", picked, tiles32, precision=lax.Precision.HIGHEST)
    return result.reshape(width, blocks_here * BS)


def body(tiles, columns, start_vectors):
    blocks_here = tiles.shape[0]
    total_blocks = blocks_here * lax.axis_size("rows")
    first_block = lax.axis_index("rows") * blocks_here
    global_rows = first_block + jnp.arange(blocks_here, dtype=jnp.int32)
    offsets = jnp.mod(columns - global_rows[:, None] + HB, total_blocks)
    slots = jnp.arange(blocks_here, dtype=jnp.int32)[:, None] + offsets
    tiles32 = tiles.astype(jnp.float32)
    previous = start_vectors
    current = operate(start_vectors, tiles32, slots)
    for step in range(STEPS - 1):
        following = 2.0 * operate(current, tiles32, slots) - previous
        previous = current
        current = following
    scale = jnp.sqrt(jnp.float32(total_blocks * BS))
    width = current.shape[0]
    gathered = lax.all_gather(current, "vecs", axis=0, tiled=True)
    partial_rows = jnp.einsum("mn,kn->mk", current, gathered, precision=lax.Precision.HIGHEST)
    summed_rows = lax.psum(partial_rows, "rows")
    gram = lax.all_gather(summed_rows, "vecs", axis=0, tiled=True)
    factor = jnp.linalg.cholesky(gram)
    solved_all = lax.linalg.triangular_solve(factor, gathered, left_side=True, lower=True)
    own_rows = lax.dynamic_slice_in_dim(solved_all, lax.axis_index("vecs") * width, width, 0)
    return own_rows * scale


def solution(mesh):
    placed = (P("rows", None, None, None), P("rows", None), P("vecs", "rows"))
    return jax.shard_map(
        body, mesh=mesh, in_specs=placed, out_specs=P("vecs", "rows"), check_vma=False
    )
```

profile of v0, /device:TPU:1, one launch (start us, length us, event | category | flops | bytes accessed | tf_op | source)
XLA Modules:
  0.0 663.2 jit_solution(6963976007546945861)
XLA Ops:
  7.6 4.8 collective-permute-start
  12.4 10.8 %collective-permute-start.1 = (f32[64,384]{1,0:T(8,128)S(1)}, f32[64,384]{1,0:T(8,128)S(1)}, u32[]{:S(2)}, u32[]{:S(2)}) collective-permute-start(f32[64,384]{1,0:T(8,128)S(1)} %get-tuple-element.55), channel_id=1, source_target_pairs={{16,0},{32,16},{48,32},{64,48},{80,64},{96,80},{112,96},{128,112},... | collective-permute-start | bytes 294920 | tf_op jit(solution)/shard_map/ppermute | solution.py:19
  27.4 1.9 collective-permute-start.2
  29.3 7.1 %collective-permute-start.3 = (f32[64,384]{1,0:T(8,128)S(1)}, f32[64,384]{1,0:T(8,128)S(1)}, u32[]{:S(2)}, u32[]{:S(2)}) collective-permute-start(f32[64,384]{1,0:T(8,128)S(1)} %get-tuple-element.53), channel_id=1, source_target_pairs={{16,0},{32,16},{48,32},{64,48},{80,64},{96,80},{112,96},{128,112},... | collective-permute-start | bytes 294920 | tf_op jit(solution)/shard_map/ppermute | solution.py:19
  36.4 1.6 collective-permute-done.3
  39.6 1.9 collective-permute-start.4
  41.5 7.1 %collective-permute-start.5 = (f32[64,384]{1,0:T(8,128)S(1)}, f32[64,384]{1,0:T(8,128)S(1)}, u32[]{:S(2)}, u32[]{:S(2)}) collective-permute-start(f32[64,384]{1,0:T(8,128)S(1)} %get-tuple-element.51), channel_id=1, source_target_pairs={{16,0},{32,16},{48,32},{64,48},{80,64},{96,80},{112,96},{128,112},... | collective-permute-start | bytes 294920 | tf_op jit(solution)/shard_map/ppermute | solution.py:19
  48.6 1.6 collective-permute-done.5
  51.8 1.9 collective-permute-start.6
  53.7 7.1 %collective-permute-start.7 = (f32[64,384]{1,0:T(8,128)S(1)}, f32[64,384]{1,0:T(8,128)S(1)}, u32[]{:S(2)}, u32[]{:S(2)}) collective-permute-start(f32[64,384]{1,0:T(8,128)S(1)} %get-tuple-element.49), channel_id=1, source_target_pairs={{16,0},{32,16},{48,32},{64,48},{80,64},{96,80},{112,96},{128,112},... | collective-permute-start | bytes 294920 | tf_op jit(solution)/shard_map/ppermute | solution.py:19
  60.9 1.6 collective-permute-done.7
  64.7 45.6 %all-gather.3.cloned.1.call-done = f32[1024,512]{1,0:T(8,128)} async-done(((f32[64,512]{1,0:T(8,128)}), f32[1024,512]{1,0:T(8,128)}) %all-gather.3.cloned.1.call-update) | async-done | bytes 2097168 | tf_op jit(solution)/shard_map/all_gather | solution.py:50
  110.4 4.5 fusion.74
  114.9 149.6 %all-reduce.3.cloned.1.call-done = f32[64,1024]{1,0:T(8,128)} async-done(((f32[64,1024]{1,0:T(8,128)}), f32[64,1024]{1,0:T(8,128)}) %all-reduce.3.cloned.1.call-update) | async-done | bytes 262160 | tf_op jit(solution)/shard_map/psum | solution.py:52
  264.6 48.1 %all-gather.5.cloned.1.call-done = f32[1024,1024]{1,0:T(8,128)} async-done(((f32[64,1024]{1,0:T(8,128)}), f32[1024,1024]{1,0:T(8,128)}) %all-gather.5.cloned.1.call-update) | async-done | bytes 4194320 | tf_op jit(solution)/shard_map/all_gather | solution.py:53
  312.7 5.8 copy.26
  318.5 4.4 fusion
  323.0 1.9 copy-done.1
  324.9 11.7 %cholesky.223 = f32[128,128]{1,0:T(8,128)S(1)} custom-call(f32[128,128]{1,0:T(8,128)S(1)} %cholesky.580), custom_call_target="Cholesky" | custom-call | tf_op jit(solution)/shard_map/jit(cholesky)/cholesky | solution.py:54
  336.6 9.8 %custom-call.62 = f32[1,128,128]{1,2,0:T(8,128)S(1)} custom-call(f32[1,128,128]{2,1,0:T(8,128)S(1)} %get-tuple-element.77), custom_call_target="InvertDiagBlocksLowerTriangular" | custom-call | tf_op jit(solution)/shard_map/jit(cholesky)/cholesky | solution.py:54
  346.5 2.5 cholesky.255
  349.0 2.4 constant_dynamic-update-slice_fusion.32
  351.3 1.5 convolution_subtract_fusion
  352.9 11.9 %cholesky.244 = f32[128,128]{1,0:T(8,128)S(1)} custom-call(f32[128,128]{1,0:T(8,128)S(1)} %cholesky.584), custom_call_target="Cholesky" | custom-call | tf_op jit(solution)/shard_map/jit(cholesky)/cholesky | solution.py:54
  365.4 9.8 %custom-call.63 = f32[1,128,128]{1,2,0:T(8,128)S(1)} custom-call(f32[1,128,128]{2,1,0:T(8,128)S(1)} %get-tuple-element.74), custom_call_target="InvertDiagBlocksLowerTriangular" | custom-call | tf_op jit(solution)/shard_map/jit(cholesky)/cholesky | solution.py:54
  375.2 1.2 convolution_dynamic-update-slice_fusion
  376.5 2.1 convolution_subtract_fusion.1
  378.6 11.7 %cholesky.468 = f32[128,128]{1,0:T(8,128)S(1)} custom-call(f32[128,128]{1,0:T(8,128)S(1)} %cholesky.589), custom_call_target="Cholesky" | custom-call | tf_op jit(solution)/shard_map/jit(cholesky)/cholesky | solution.py:54
  391.5 9.8 %custom-call.64 = f32[1,128,128]{1,2,0:T(8,128)S(1)} custom-call(f32[1,128,128]{2,1,0:T(8,128)S(1)} %get-tuple-element.71), custom_call_target="InvertDiagBlocksLowerTriangular" | custom-call | tf_op jit(solution)/shard_map/jit(cholesky)/cholesky | solution.py:54
  401.3 1.2 convolution_dynamic-update-slice_fusion.1
  402.5 2.3 convolution_subtract_fusion.2
  404.9 11.9 %cholesky.487 = f32[128,128]{1,0:T(8,128)S(1)} custom-call(f32[128,128]{1,0:T(8,128)S(1)} %cholesky.594), custom_call_target="Cholesky" | custom-call | tf_op jit(solution)/shard_map/jit(cholesky)/cholesky | solution.py:54
  418.0 9.8 %custom-call.65 = f32[1,128,128]{1,2,0:T(8,128)S(1)} custom-call(f32[1,128,128]{2,1,0:T(8,128)S(1)} %get-tuple-element.68), custom_call_target="InvertDiagBlocksLowerTriangular" | custom-call | tf_op jit(solution)/shard_map/jit(cholesky)/cholesky | solution.py:54
  427.9 1.1 convolution_dynamic-update-slice_fusion.3
  429.0 2.3 convolution_subtract_fusion.10
  431.3 11.7 %cholesky.506 = f32[128,128]{1,0:T(8,128)S(1)} custom-call(f32[128,128]{1,0:T(8,128)S(1)} %cholesky.599), custom_call_target="Cholesky" | custom-call | tf_op jit(solution)/shard_map/jit(cholesky)/cholesky | solution.py:54
  444.4 10.2 %custom-call.66 = f32[1,128,128]{1,2,0:T(8,128)S(1)} custom-call(f32[1,128,128]{2,1,0:T(8,128)S(1)} %get-tuple-element.65), custom_call_target="InvertDiagBlocksLowerTriangular" | custom-call | tf_op jit(solution)/shard_map/jit(cholesky)/cholesky | solution.py:54
  454.6 1.0 convolution_dynamic-update-slice_fusion.4
  455.6 2.3 convolution_subtract_fusion.11
  457.9 11.7 %cholesky.526 = f32[128,128]{1,0:T(8,128)S(1)} custom-call(f32[128,128]{1,0:T(8,128)S(1)} %cholesky.604), custom_call_target="Cholesky" | custom-call | tf_op jit(solution)/shard_map/jit(cholesky)/cholesky | solution.py:54
  470.9 9.8 %custom-call.67 = f32[1,128,128]{1,2,0:T(8,128)S(1)} custom-call(f32[1,128,128]{2,1,0:T(8,128)S(1)} %get-tuple-element.62), custom_call_target="InvertDiagBlocksLowerTriangular" | custom-call | tf_op jit(solution)/shard_map/jit(cholesky)/cholesky | solution.py:54
  481.6 2.0 convolution_subtract_fusion.12
  483.7 11.9 %cholesky.546 = f32[128,128]{1,0:T(8,128)S(1)} custom-call(f32[128,128]{1,0:T(8,128)S(1)} %cholesky.609), custom_call_target="Cholesky" | custom-call | tf_op jit(solution)/shard_map/jit(cholesky)/cholesky | solution.py:54
  496.8 9.8 %custom-call.68 = f32[1,128,128]{1,2,0:T(8,128)S(1)} custom-call(f32[1,128,128]{2,1,0:T(8,128)S(1)} %get-tuple-element.59), custom_call_target="InvertDiagBlocksLowerTriangular" | custom-call | tf_op jit(solution)/shard_map/jit(cholesky)/cholesky | solution.py:54
  507.5 1.8 convolution_subtract_fusion.13
  509.3 11.7 %cholesky.564 = f32[128,128]{1,0:T(8,128)S(1)} custom-call(f32[128,128]{1,0:T(8,128)S(1)} %convolution_subtract_fusion.13), custom_call_target="Cholesky" | custom-call | tf_op jit(solution)/shard_map/jit(cholesky)/cholesky | solution.py:54
  528.0 4.9 select_select_fusion
  532.9 27.6 %while.1 = (s32[]{:T(128)}, f32[1024,1024]{1,0:T(8,128)}, s32[8,2]{0,1:T(2,128)S(1)}, f32[8,128,128]{2,1,0:T(8,128)}, s32[]{:T(128)}) while((s32[]{:T(128)}, f32[1024,1024]{1,0:T(8,128)}, s32[8,2]{0,1:T(2,128)S(1)}, f32[8,128,128]{2,1,0:T(8,128)}, s32[]{:T(128)}) %tuple.61), condition=%wide.while_cond, body=%wide.while_body.sunk | while | flops 2 | bytes 132205 | solution.py:55
  533.5 2.8 bitcast_dynamic-update-slice_fusion.2
  537.0 2.8 bitcast_dynamic-update-slice_fusion.2
  540.5 2.8 bitcast_dynamic-update-slice_fusion.2
  543.9 2.8 bitcast_dynamic-update-slice_fusion.2
  547.4 2.8 bitcast_dynamic-update-slice_fusion.2
  550.9 2.8 bitcast_dynamic-update-slice_fusion.2
  554.3 2.8 bitcast_dynamic-update-slice_fusion.2
  557.8 2.8 bitcast_dynamic-update-slice_fusion.2
  560.6 79.6 %custom-call.69 = f32[8,128,128]{1,2,0:T(8,128)S(1)} custom-call(f32[8,128,128]{2,1,0:T(8,128)} %get-tuple-element.12), custom_call_target="InvertDiagBlocksLowerTriangular" | custom-call | tf_op jit(solution)/shard_map/triangular_solve | solution.py:55
  640.7 1.2 convolution_subtract_fusion.6
  642.4 1.3 convolution_subtract_fusion.5
  644.2 1.6 convolution_subtract_fusion.8
  646.2 1.7 convolution_subtract_fusion.9
  648.4 1.9 convolution_subtract_fusion.4
  650.7 2.0 convolution_subtract_fusion.7
  653.1 2.2 convolution_subtract_fusion.3
  (94 shorter events, 31.1 us)
Async XLA Ops:
  6.5 19.8 %copy-start = (bf16[4,6,128,128]{3,2,1,0:T(8,128)(2,1)S(1)}, bf16[4,6,128,128]{3,2,1,0:T(8,128)(2,1)}, u32[]{:S(2)}) copy-start(bf16[4,6,128,128]{3,2,1,0:T(8,128)(2,1)} %param.3) | copy-start | bytes 2359300
  6.5 103.8 %all-gather.3.cloned.1.call-start = ((), (), s32[]{:S(2)}) async-start(), calls=%async_computation | async-start | bytes 2228224 | tf_op jit(solution)/shard_map/all_gather | solution.py:50
  7.6 16.5 %collective-permute-start = (f32[64,384]{1,0:T(8,128)S(1)}, f32[64,384]{1,0:T(8,128)S(1)}, u32[]{:S(2)}, u32[]{:S(2)}) collective-permute-start(f32[64,384]{1,0:T(8,128)S(1)} %get-tuple-element.54), channel_id=1, source_target_pairs={{0,16},{16,32},{32,48},{48,64},{64,80},{80,96},{96,112},{112,128},... | collective-permute-start | bytes 294920 | tf_op jit(solution)/shard_map/ppermute | solution.py:18
  12.4 12.4 %collective-permute-start.1 = (f32[64,384]{1,0:T(8,128)S(1)}, f32[64,384]{1,0:T(8,128)S(1)}, u32[]{:S(2)}, u32[]{:S(2)}) collective-permute-start(f32[64,384]{1,0:T(8,128)S(1)} %get-tuple-element.55), channel_id=1, source_target_pairs={{16,0},{32,16},{48,32},{64,48},{80,64},{96,80},{112,96},{128,112},... | collective-permute-start | bytes 294920 | tf_op jit(solution)/shard_map/ppermute | solution.py:19
  25.7 13.8 %copy-start.3 = (f32[64,512]{1,0:T(8,128)S(1)}, f32[64,512]{1,0:T(8,128)}, u32[]{:S(2)}) copy-start(f32[64,512]{1,0:T(8,128)} %param.5) | copy-start | bytes 393220
  27.4 9.1 %collective-permute-start.2 = (f32[64,384]{1,0:T(8,128)S(1)}, f32[64,384]{1,0:T(8,128)S(1)}, u32[]{:S(2)}, u32[]{:S(2)}) collective-permute-start(f32[64,384]{1,0:T(8,128)S(1)} %get-tuple-element.52), channel_id=1, source_target_pairs={{0,16},{16,32},{32,48},{48,64},{64,80},{80,96},{96,112},{112,128},... | collective-permute-start | bytes 294920 | tf_op jit(solution)/shard_map/ppermute | solution.py:18
  29.3 8.7 %collective-permute-start.3 = (f32[64,384]{1,0:T(8,128)S(1)}, f32[64,384]{1,0:T(8,128)S(1)}, u32[]{:S(2)}, u32[]{:S(2)}) collective-permute-start(f32[64,384]{1,0:T(8,128)S(1)} %get-tuple-element.53), channel_id=1, source_target_pairs={{16,0},{32,16},{48,32},{64,48},{80,64},{96,80},{112,96},{128,112},... | collective-permute-start | bytes 294920 | tf_op jit(solution)/shard_map/ppermute | solution.py:19
  39.6 9.1 %collective-permute-start.4 = (f32[64,384]{1,0:T(8,128)S(1)}, f32[64,384]{1,0:T(8,128)S(1)}, u32[]{:S(2)}, u32[]{:S(2)}) collective-permute-start(f32[64,384]{1,0:T(8,128)S(1)} %get-tuple-element.50), channel_id=1, source_target_pairs={{0,16},{16,32},{32,48},{48,64},{64,80},{80,96},{96,112},{112,128},... | collective-permute-start | bytes 294920 | tf_op jit(solution)/shard_map/ppermute | solution.py:18
  41.5 8.7 %collective-permute-start.5 = (f32[64,384]{1,0:T(8,128)S(1)}, f32[64,384]{1,0:T(8,128)S(1)}, u32[]{:S(2)}, u32[]{:S(2)}) collective-permute-start(f32[64,384]{1,0:T(8,128)S(1)} %get-tuple-element.51), channel_id=1, source_target_pairs={{16,0},{32,16},{48,32},{64,48},{80,64},{96,80},{112,96},{128,112},... | collective-permute-start | bytes 294920 | tf_op jit(solution)/shard_map/ppermute | solution.py:19
  51.8 9.1 %collective-permute-start.6 = (f32[64,384]{1,0:T(8,128)S(1)}, f32[64,384]{1,0:T(8,128)S(1)}, u32[]{:S(2)}, u32[]{:S(2)}) collective-permute-start(f32[64,384]{1,0:T(8,128)S(1)} %get-tuple-element.48), channel_id=1, source_target_pairs={{0,16},{16,32},{32,48},{48,64},{64,80},{80,96},{96,112},{112,128},... | collective-permute-start | bytes 294920 | tf_op jit(solution)/shard_map/ppermute | solution.py:18
  53.7 8.7 %collective-permute-start.7 = (f32[64,384]{1,0:T(8,128)S(1)}, f32[64,384]{1,0:T(8,128)S(1)}, u32[]{:S(2)}, u32[]{:S(2)}) collective-permute-start(f32[64,384]{1,0:T(8,128)S(1)} %get-tuple-element.49), channel_id=1, source_target_pairs={{16,0},{32,16},{48,32},{64,48},{80,64},{96,80},{112,96},{128,112},... | collective-permute-start | bytes 294920 | tf_op jit(solution)/shard_map/ppermute | solution.py:19
  64.7 199.8 %all-reduce.3.cloned.1.call-start = ((), (), s32[]{:S(2)}) async-start(), calls=%async_computation.1 | async-start | bytes 524288 | tf_op jit(solution)/shard_map/psum | solution.py:52
  114.9 197.8 %all-gather.5.cloned.1.call-start = ((), (), s32[]{:S(2)}) async-start(), calls=%async_computation.2 | async-start | bytes 4456448 | tf_op jit(solution)/shard_map/all_gather | solution.py:53
  323.0 1.9 copy-start.1
  528.0 112.2 %copy-start.2 = (f32[1024,512]{1,0:T(8,128)S(1)}, f32[1024,512]{1,0:T(8,128)}, u32[]{:S(2)}) copy-start(f32[1024,512]{1,0:T(8,128)} %all-gather.3.cloned.1.call-done) | copy-start | bytes 6291460
Sparse Core Ops, SparseCore 0:
  64.8 45.4 all-gather.2
  115.0 149.5 all-reduce.2
  266.7 45.9 all-gather.4
where the time goes:
time: 669 us; the launch traced here: 663 us
  other arithmetic  264 us (39%)
  waiting for transfers between devices  249 us (37%)
  matrix products  46.7 us (7%)
  starting transfers between devices  42.6 us (6%)
  local copies, waits for them, and re-layouts  41.5 us (6%)
  between operations  18.9 us (3%)
    another operation x30, other arithmetic, body(): factor = jnp.linalg.cholesky(gram)  172 us
    psum x1, waiting for transfers between devices, body(): summed_rows = lax.psum(partial_rows, 'rows')  150 us
    another operation x3, other arithmetic, body(): lax.linalg.triangular_solve(factor, gathered, left_side=True, lower=True)  84.6 us
    all_gather x1, waiting for transfers between devices, body(): gram = lax.all_gather(summed_rows, 'vecs', axis=0, tiled=True)  48.1 us
    all_gather x1, waiting for transfers between devices, body(): gathered = lax.all_gather(current, 'vecs', axis=0, tiled=True)  45.6 us
    ppermute x4, starting transfers between devices, with_halo(): after = lax.ppermute(initial, axis, down)  32 us
    another operation x24, local copies, waits for them, and re-layouts  27.6 us
    another operation x14, matrix products, body(): factor = jnp.linalg.cholesky(gram)  23.1 us
  transfers between devices with their start and end apart: 11, of which 10 were waited for; matrix products, arithmetic and copies ran while one was open for 0% of the time, Pallas kernels for 0%

commit v1 on v0

v1 whole, which is shorter than its diff:
```python
import functools

import jax
import jax.numpy as jnp
from jax import lax
from jax.experimental import pallas as pl
from jax.experimental.pallas import tpu as pltpu
from jax.sharding import PartitionSpec as P

f32, bf16 = jnp.float32, jnp.bfloat16
M, BS, NB, GR = 1024, 128, 8, 8


def split(x):
    hi = x.astype(bf16)
    return hi, (x - hi.astype(f32)).astype(bf16)


def mm(a, b, tb):
    dims = (((1,), (1 if tb else 0,)), ((), ()))
    return lax.dot_general(a, b, dims, preferred_element_type=f32)


def mm3(a, b, tb=False):
    return mm(a[0], b[0], tb) + (mm(a[0], b[1], tb) + mm(a[1], b[0], tb))


def recip(x):
    r = pl.reciprocal(x, approx=True)
    return r * (2.0 - x * r)


def diag_factor(a_ref, w_ref):
    lane = lax.broadcasted_iota(jnp.int32, (8, BS), 1)
    sub = lax.broadcasted_iota(jnp.int32, (8, BS), 0)
    for g in range(BS // GR):
        lo = g * GR
        ing = (lane >= lo) & (lane < lo + GR)
        p = a_ref[lo:lo + 8, :]
        cols = [jnp.broadcast_to(p[:, lo + j:lo + j + 1], (8, BS)) for j in range(GR)]
        x = jnp.where(lane == sub + lo, 1.0, jnp.where(ing, 0.0, p))
        w = x
        for j in range(0, GR, 2):
            cj, ck = cols[j], cols[j + 1]

            def row(v, i):
                return jnp.broadcast_to(v[i:i + 1, :], (8, BS))
            a, b, c = row(cj, j), row(cj, j + 1), row(ck, j + 1)
            det = a * c - b * b
            pair = (sub == j) | (sub == j + 1)
            cjm = jnp.where(sub == j, -1.0, jnp.where(sub == j + 1, 0.0, cj))
            ckm = jnp.where(sub == j + 1, -1.0, jnp.where(sub == j, 0.0, ck))
            r = recip(det)
            x0, x1 = row(x, j), row(x, j + 1)
            y1 = a * x1 - b * x0
            w = jnp.where(sub == j, x0 * lax.rsqrt(a), jnp.where(sub == j + 1, y1 * lax.rsqrt(a * det), w))
            for m in list(range(j + 2, GR)) + [-1]:
                v = x if m < 0 else cols[m]
                v0, v1 = row(v, j), row(v, j + 1)
                y0 = c * v0 - b * v1
                y1 = a * v1 - b * v0
                z = cjm * y0 + ckm * y1
                new = jnp.where(pair, 0.0, v) - r * z
                if m < 0:
                    x = new
                else:
                    cols[m] = new
        w_ref[lo:lo + 8, :] = jnp.where(lane < lo + GR, w, 0.0)
        for h in range(g + 1, BS // GR):
            q = a_ref[h * 8:h * 8 + 8, :]
            cs = [jnp.broadcast_to(q[:, lo + j:lo + j + 1], (8, BS)) for j in range(GR)]
            t = [cs[j] * jnp.broadcast_to(x[j:j + 1, :], (8, BS)) for j in range(GR)]
            while len(t) > 1:
                t = [t[i] + t[i + 1] for i in range(0, len(t), 2)]
            a_ref[h * 8:h * 8 + 8, :] = jnp.where(ing, 0.0, q) - t[0]


def kernel(n_root, v_ref, g_ref, f_ref, o_ref, a_ref, w_ref, whi, wlo, lhi, llo, scol, srow, r_ref, xhi, xlo):
    eye = lax.broadcasted_iota(jnp.int32, (BS, BS), 0) == lax.broadcasted_iota(jnp.int32, (BS, BS), 1)
    for k in range(NB):
        d = jnp.where(eye, g_ref[k * BS:(k + 1) * BS, k * BS:(k + 1) * BS], 0.0)
        srow[:, k * BS:(k + 1) * BS] = jnp.broadcast_to(lax.rsqrt(jnp.sum(d, axis=0, keepdims=True)), (8, BS))
        scol[k * BS:(k + 1) * BS, :] = jnp.broadcast_to(lax.rsqrt(jnp.sum(d, axis=1, keepdims=True)), (BS, BS))

    def column(k):
        s = g_ref[k * BS:, k * BS:(k + 1) * BS] * scol[k * BS:, :] * srow[0:1, k * BS:(k + 1) * BS]
        if k:
            rows = (lhi[k * BS:, :k * BS], llo[k * BS:, :k * BS])
            own = (lhi[k * BS:(k + 1) * BS, :k * BS], llo[k * BS:(k + 1) * BS, :k * BS])
            s = s - mm3(rows, own, True)
        return s

    a_ref[...] = column(0)

    def after(k):
        hi, lo = split(w_ref[...])
        whi[k], wlo[k] = hi, lo
        if k + 1 == NB:
            return
        h, l = split(mm3(split(a_ref[BS:M - k * BS, :]), (hi, lo), True))
        lhi[(k + 1) * BS:, k * BS:(k + 1) * BS] = h
        llo[(k + 1) * BS:, k * BS:(k + 1) * BS] = l
        a_ref[0:M - (k + 1) * BS, :] = column(k + 1)

    def step(k, _):
        diag_factor(a_ref, w_ref)
        for kk in range(NB):
            @pl.when(k == kk)
            def _():
                after(kk)
        return 0
    lax.fori_loop(0, NB, step, 0)
    v = v_ref[0]
    sel = lax.broadcasted_iota(jnp.int32, (64, M), 0) + v * 64 == lax.broadcasted_iota(jnp.int32, (64, M), 1)
    r_ref[...] = jnp.where(sel, f32(n_root), 0.0)
    for k in range(NB - 1, -1, -1):
        cur = mm3(split(r_ref[:, k * BS:(k + 1) * BS]), (whi[k], wlo[k]))
        if k:
            x = split(cur)
            r_ref[:, :k * BS] -= mm3(x, (lhi[k * BS:(k + 1) * BS, :k * BS], llo[k * BS:(k + 1) * BS, :k * BS]))
        h, l = split(cur * srow[0:1, k * BS:(k + 1) * BS])
        xhi[:, k * BS:(k + 1) * BS] = h
        xlo[:, k * BS:(k + 1) * BS] = l
    o_ref[...] = mm3((xhi[...], xlo[...]), split(f_ref[...]))


def k2(v, g, f, n_root=128.0):
    vm = pl.BlockSpec(memory_space=pltpu.VMEM)
    return pl.pallas_call(
        functools.partial(kernel, n_root),
        out_shape=jax.ShapeDtypeStruct((64, 512), f32),
        in_specs=[pl.BlockSpec(memory_space=pltpu.SMEM), vm, vm],
        out_specs=vm,
        scratch_shapes=[
            pltpu.VMEM((M, BS), f32), pltpu.VMEM((BS, BS), f32),
            pltpu.VMEM((NB, BS, BS), bf16), pltpu.VMEM((NB, BS, BS), bf16),
            pltpu.VMEM((M, M), bf16), pltpu.VMEM((M, M), bf16),
            pltpu.VMEM((M, BS), f32), pltpu.VMEM((8, M), f32),
            pltpu.VMEM((64, M), f32), pltpu.VMEM((64, M), bf16), pltpu.VMEM((64, M), bf16)],
        compiler_params=pltpu.CompilerParams(vmem_limit_bytes=48 << 20),
    )(v, g, f)

HB = 3
STEPS = 4


def with_halo(shard, sides, width):
    for axis, dim in sides:
        devices, length = (lax.axis_size(axis), shard.shape[dim])
        up = [(i, (i + 1) % devices) for i in range(devices)]
        down = [(j, i) for i, j in up]
        last = lax.slice_in_dim(shard, length - width, length, axis=dim)
        initial = lax.slice_in_dim(shard, 0, width, axis=dim)
        before = lax.ppermute(last, axis, up)
        after = lax.ppermute(initial, axis, down)
        shard = jnp.concatenate([before, shard, after], axis=dim)
    return shard


def operate(field, band):
    extended = with_halo(field, (("rows", 1),), HB * BS)
    parts = [
        jnp.einsum("mj,ji->mi", extended[:, b * BS:(b + 2 * HB + 1) * BS], band[b], precision=lax.Precision.HIGHEST)
        for b in range(band.shape[0])
    ]
    return jnp.concatenate(parts, axis=1)


def body(tiles, columns, start_vectors):
    blocks_here = tiles.shape[0]
    total_blocks = blocks_here * lax.axis_size("rows")
    first_block = lax.axis_index("rows") * blocks_here
    global_rows = first_block + jnp.arange(blocks_here, dtype=jnp.int32)
    offsets = jnp.mod(columns - global_rows[:, None] + HB, total_blocks)
    chosen = offsets[:, None, :] == jnp.arange(2 * HB + 1, dtype=jnp.int32)[None, :, None]
    tiles32 = jnp.swapaxes(tiles.astype(jnp.float32), 2, 3)
    band = jnp.zeros((blocks_here, 2 * HB + 1, BS, BS), jnp.float32)
    for t in range(tiles.shape[1]):
        band = band + jnp.where(chosen[:, :, t, None, None], tiles32[:, None, t], 0.0)
    band = band.reshape(blocks_here, (2 * HB + 1) * BS, BS)
    previous = start_vectors
    current = operate(start_vectors, band)
    for step in range(STEPS - 1):
        following = 2.0 * operate(current, band) - previous
        previous = current
        current = following
    width = current.shape[0]
    gathered = lax.all_gather(current, "vecs", axis=0, tiled=True)
    partial_rows = jnp.einsum("mn,kn->mk", current, gathered, precision=lax.Precision.HIGHEST)
    summed_rows = lax.psum(partial_rows, "rows")
    gram = lax.all_gather(summed_rows, "vecs", axis=0, tiled=True)
    where = lax.axis_index("vecs").astype(jnp.int32).reshape(1)
    return k2(where, gram, gathered)


def solution(mesh):
    placed = (P("rows", None, None, None), P("rows", None), P("vecs", "rows"))
    return jax.shard_map(
        body, mesh=mesh, in_specs=placed, out_specs=P("vecs", "rows"), check_vma=False
    )
```

time: 669 us -> 365 us (0.55)
  other arithmetic: 264 us -> 3.78 us
  Pallas kernels: 0 us -> 40.3 us
  local copies, waits for them, and re-layouts: 41.5 us -> 2.33 us
  matrix products: 46.7 us -> 11.3 us
    another operation x33 -> x0, other arithmetic: 257 us -> none  [the longest x30 172 us: body(): factor = jnp.linalg.cholesky(gram)]
    pallas_call x0 -> x1, Pallas kernels: none -> 40.3 us  [k2(): pl.pallas_call(functools.partial(kernel, n_root), out_shape=jax.ShapeDtyp...]
    another operation x29 -> x0, matrix products: 38.6 us -> none  [the longest x14 23.1 us: body(): factor = jnp.linalg.cholesky(gram)]
    another operation x33 -> x0, local copies, waits for them, and re-layouts: 30.2 us -> none
  transfers between devices with their start and end apart: 11 -> 11, of which waited for: 10 -> 10; matrix products, arithmetic and copies ran while one was open for 0% -> 1% of each run, Pallas kernels for 0% -> 0%
where the time goes in v1:
time: 365 us
  waiting for transfers between devices  251 us (69%)
  starting transfers between devices  42.4 us (12%)
  Pallas kernels  40.3 us (11%)
  between operations  13.4 us (4%)
  matrix products  11.3 us (3%)
  other arithmetic  3.78 us (1%)
    psum x1, waiting for transfers between devices, body(): summed_rows = lax.psum(partial_rows, 'rows')  149 us
    all_gather x1, waiting for transfers between devices, body(): gram = lax.all_gather(summed_rows, 'vecs', axis=0, tiled=True)  48.1 us
    all_gather x1, waiting for transfers between devices, body(): gathered = lax.all_gather(current, 'vecs', axis=0, tiled=True)  46.2 us
    pallas_call x1, Pallas kernels, k2(): pl.pallas_call(functools.partial(kernel, n_root), out_shape=jax.ShapeDtyp...  40.3 us
    ppermute x4, starting transfers between devices, with_halo(): after = lax.ppermute(initial, axis, down)  34.5 us
    ppermute x4, starting transfers between devices, with_halo(): before = lax.ppermute(last, axis, up)  7.68 us
  transfers between devices with their start and end apart: 11, of which 10 were waited for; matrix products, arithmetic and copies ran while one was open for 1% of the time, Pallas kernels for 0%

profile of v1, /device:TPU:1, one launch (start us, length us, event | category | flops | bytes accessed | tf_op | source)
XLA Modules:
  0.0 364.6 jit_solution(12624723449860222576)
XLA Ops:
  6.5 0.0 all-gather.3.cloned.1.call-start
  6.5 1.0 fusion.53
  7.5 13.7 %collective-permute-start.1 = (f32[64,384]{1,0:T(8,128)S(1)}, f32[64,384]{1,0:T(8,128)S(1)}, u32[]{:S(2)}, u32[]{:S(2)}) collective-permute-start(f32[64,384]{1,0:T(8,128)S(1)} %get-tuple-element.19), channel_id=1, source_target_pairs={{16,0},{32,16},{48,32},{64,48},{80,64},{96,80},{112,96},{128,112},... | collective-permute-start | bytes 294920 | tf_op jit(solution)/shard_map/ppermute | solution.py:155
  21.2 1.9 collective-permute-start
  23.2 0.8 add_select_fusion
  23.9 0.1 copy.4
  24.0 0.1 iota_compare_fusion
  24.1 1.3 convert_bitcast_fusion
  25.4 0.1 slice_bitcast_fusion.5
  25.6 0.1 copy.5
  25.7 0.1 copy.10
  25.8 0.1 copy.9
  26.0 0.1 copy.8
  26.1 0.1 copy.7
  26.3 0.1 copy.6
  26.4 0.9 select_add_fusion
  27.3 0.0 copy-start.1
  27.3 0.2 fusion.50
  27.5 2.4 collective-permute-done
  29.9 0.0 copy-done.1
  29.9 0.0 collective-permute-done.1
  30.0 0.4 fusion.12
  30.4 0.4 fusion.14
  30.8 0.4 fusion.16
  31.2 0.4 fusion.20
  31.7 1.9 collective-permute-start.2
  33.6 6.7 %collective-permute-start.3 = (f32[64,384]{1,0:T(8,128)S(1)}, f32[64,384]{1,0:T(8,128)S(1)}, u32[]{:S(2)}, u32[]{:S(2)}) collective-permute-start(f32[64,384]{1,0:T(8,128)S(1)} %get-tuple-element.26), channel_id=1, source_target_pairs={{16,0},{32,16},{48,32},{64,48},{80,64},{96,80},{112,96},{128,112},... | collective-permute-start | bytes 294920 | tf_op jit(solution)/shard_map/ppermute | solution.py:155
  40.3 0.1 collective-permute-done.2
  40.4 1.5 collective-permute-done.3
  41.9 0.4 fusion.8
  42.3 0.4 fusion.10
  42.8 0.4 fusion.54
  43.2 0.4 fusion.55
  43.7 1.9 collective-permute-start.4
  45.6 7.1 %collective-permute-start.5 = (f32[64,384]{1,0:T(8,128)S(1)}, f32[64,384]{1,0:T(8,128)S(1)}, u32[]{:S(2)}, u32[]{:S(2)}) collective-permute-start(f32[64,384]{1,0:T(8,128)S(1)} %get-tuple-element.18), channel_id=1, source_target_pairs={{16,0},{32,16},{48,32},{64,48},{80,64},{96,80},{112,96},{128,112},... | collective-permute-start | bytes 294920 | tf_op jit(solution)/shard_map/ppermute | solution.py:155
  52.6 0.1 collective-permute-done.4
  52.7 1.6 collective-permute-done.5
  54.3 0.4 fusion.4
  54.7 0.4 fusion.6
  55.1 0.4 fusion.24
  55.6 0.4 fusion.28
  56.0 1.9 collective-permute-start.6
  58.0 7.1 %collective-permute-start.7 = (f32[64,384]{1,0:T(8,128)S(1)}, f32[64,384]{1,0:T(8,128)S(1)}, u32[]{:S(2)}, u32[]{:S(2)}) collective-permute-start(f32[64,384]{1,0:T(8,128)S(1)} %get-tuple-element.16), channel_id=1, source_target_pairs={{16,0},{32,16},{48,32},{64,48},{80,64},{96,80},{112,96},{128,112},... | collective-permute-start | bytes 294920 | tf_op jit(solution)/shard_map/ppermute | solution.py:155
  65.0 0.1 collective-permute-done.6
  65.1 1.6 collective-permute-done.7
  66.7 0.4 fusion
  67.1 0.4 fusion.2
  67.5 0.4 fusion.32
  67.9 0.4 fusion.36
  68.3 0.7 fusion.42
  69.0 0.0 all-gather.3.cloned.1.call-update
  69.0 0.0 all-reduce.2.cloned.1.call-start
  69.1 46.2 %all-gather.3.cloned.1.call-done.f_ref = f32[1024,512]{1,0:T(8,128)} async-done(((f32[64,512]{1,0:T(8,128)}), f32[1024,512]{1,0:T(8,128)}) %all-gather.3.cloned.1.call-update) | async-done | bytes 2097168 | tf_op jit(solution)/shard_map/all_gather | solution.py:188
  115.3 0.0 copy-start
  115.3 4.6 %fusion.56 = f32[64,1024]{1,0:T(8,128)} fusion(f32[64,512]{1,0:T(8,128)} %fusion.42, f32[1024,512]{1,0:T(8,128)} %all-gather.3.cloned.1.call-done.f_ref), kind=kOutput, calls=%fused_computation.101 | convolution fusion | flops 402653184 | bytes 2490368 | tf_op jit(solution)/shard_map/mn,kn->mk/dot_general | solution.py:189
  119.9 0.0 all-reduce.2.cloned.1.call-update
  119.9 0.2 all-gather.5.cloned.1.call-start
  120.1 149.4 %all-reduce.2.cloned.1.call-done = f32[64,1024]{1,0:T(8,128)} async-done(((f32[64,1024]{1,0:T(8,128)}), f32[64,1024]{1,0:T(8,128)}) %all-reduce.2.cloned.1.call-update) | async-done | bytes 262160 | tf_op jit(solution)/shard_map/psum | solution.py:190
  269.6 0.0 all-gather.5.cloned.1.call-update
  269.6 48.1 %all-gather.5.cloned.1.call-done.g_ref = f32[1024,1024]{1,0:T(8,128)} async-done(((f32[64,1024]{1,0:T(8,128)}), f32[1024,1024]{1,0:T(8,128)}) %all-gather.5.cloned.1.call-update) | async-done | bytes 4194320 | tf_op jit(solution)/shard_map/all_gather | solution.py:191
  317.7 0.0 copy-done
  317.7 40.3 %shard_map.37 = f32[64,512]{1,0:T(8,128)} custom-call(s32[1]{0:T(128)} %bitcast.v_ref, f32[1024,1024]{1,0:T(8,128)} %all-gather.5.cloned.1.call-done.g_ref, f32[1024,512]{1,0:T(8,128)S(1)} %copy-done), custom_call_target="tpu_custom_call" | custom-call | tf_op jit(solution)/shard_map/pallas_call | solution.py:129
  (18 shorter events, 0.2 us)
Async XLA Ops:
  6.5 108.7 %all-gather.3.cloned.1.call-start = ((), (), s32[]{:S(2)}) async-start(), calls=%async_computation | async-start | bytes 2228224 | tf_op jit(solution)/shard_map/all_gather | solution.py:188
  7.5 22.4 %collective-permute-start.1 = (f32[64,384]{1,0:T(8,128)S(1)}, f32[64,384]{1,0:T(8,128)S(1)}, u32[]{:S(2)}, u32[]{:S(2)}) collective-permute-start(f32[64,384]{1,0:T(8,128)S(1)} %get-tuple-element.19), channel_id=1, source_target_pairs={{16,0},{32,16},{48,32},{64,48},{80,64},{96,80},{112,96},{128,112},... | collective-permute-start | bytes 294920 | tf_op jit(solution)/shard_map/ppermute | solution.py:155
  21.2 8.7 %collective-permute-start = (f32[64,384]{1,0:T(8,128)S(1)}, f32[64,384]{1,0:T(8,128)S(1)}, u32[]{:S(2)}, u32[]{:S(2)}) collective-permute-start(f32[64,384]{1,0:T(8,128)S(1)} %get-tuple-element.20), channel_id=1, source_target_pairs={{0,16},{16,32},{32,48},{48,64},{64,80},{80,96},{96,112},{112,128},... | collective-permute-start | bytes 294920 | tf_op jit(solution)/shard_map/ppermute | solution.py:154
  27.3 2.6 copy-start.1
  31.7 8.7 %collective-permute-start.2 = (f32[64,384]{1,0:T(8,128)S(1)}, f32[64,384]{1,0:T(8,128)S(1)}, u32[]{:S(2)}, u32[]{:S(2)}) collective-permute-start(f32[64,384]{1,0:T(8,128)S(1)} %get-tuple-element.25), channel_id=1, source_target_pairs={{0,16},{16,32},{32,48},{48,64},{64,80},{80,96},{96,112},{112,128},... | collective-permute-start | bytes 294920 | tf_op jit(solution)/shard_map/ppermute | solution.py:154
  33.6 8.3 %collective-permute-start.3 = (f32[64,384]{1,0:T(8,128)S(1)}, f32[64,384]{1,0:T(8,128)S(1)}, u32[]{:S(2)}, u32[]{:S(2)}) collective-permute-start(f32[64,384]{1,0:T(8,128)S(1)} %get-tuple-element.26), channel_id=1, source_target_pairs={{16,0},{32,16},{48,32},{64,48},{80,64},{96,80},{112,96},{128,112},... | collective-permute-start | bytes 294920 | tf_op jit(solution)/shard_map/ppermute | solution.py:155
  43.7 9.1 %collective-permute-start.4 = (f32[64,384]{1,0:T(8,128)S(1)}, f32[64,384]{1,0:T(8,128)S(1)}, u32[]{:S(2)}, u32[]{:S(2)}) collective-permute-start(f32[64,384]{1,0:T(8,128)S(1)} %get-tuple-element.17), channel_id=1, source_target_pairs={{0,16},{16,32},{32,48},{48,64},{64,80},{80,96},{96,112},{112,128},... | collective-permute-start | bytes 294920 | tf_op jit(solution)/shard_map/ppermute | solution.py:154
  45.6 8.7 %collective-permute-start.5 = (f32[64,384]{1,0:T(8,128)S(1)}, f32[64,384]{1,0:T(8,128)S(1)}, u32[]{:S(2)}, u32[]{:S(2)}) collective-permute-start(f32[64,384]{1,0:T(8,128)S(1)} %get-tuple-element.18), channel_id=1, source_target_pairs={{16,0},{32,16},{48,32},{64,48},{80,64},{96,80},{112,96},{128,112},... | collective-permute-start | bytes 294920 | tf_op jit(solution)/shard_map/ppermute | solution.py:155
  56.0 9.1 %collective-permute-start.6 = (f32[64,384]{1,0:T(8,128)S(1)}, f32[64,384]{1,0:T(8,128)S(1)}, u32[]{:S(2)}, u32[]{:S(2)}) collective-permute-start(f32[64,384]{1,0:T(8,128)S(1)} %get-tuple-element.15), channel_id=1, source_target_pairs={{0,16},{16,32},{32,48},{48,64},{64,80},{80,96},{96,112},{112,128},... | collective-permute-start | bytes 294920 | tf_op jit(solution)/shard_map/ppermute | solution.py:154
  58.0 8.7 %collective-permute-start.7 = (f32[64,384]{1,0:T(8,128)S(1)}, f32[64,384]{1,0:T(8,128)S(1)}, u32[]{:S(2)}, u32[]{:S(2)}) collective-permute-start(f32[64,384]{1,0:T(8,128)S(1)} %get-tuple-element.16), channel_id=1, source_target_pairs={{16,0},{32,16},{48,32},{64,48},{80,64},{96,80},{112,96},{128,112},... | collective-permute-start | bytes 294920 | tf_op jit(solution)/shard_map/ppermute | solution.py:155
  69.0 200.5 %all-reduce.2.cloned.1.call-start = ((), (), s32[]{:S(2)}) async-start(), calls=%async_computation.1 | async-start | bytes 524288 | tf_op jit(solution)/shard_map/psum | solution.py:190
  115.3 202.5 %copy-start = (f32[1024,512]{1,0:T(8,128)S(1)}, f32[1024,512]{1,0:T(8,128)}, u32[]{:S(2)}) copy-start(f32[1024,512]{1,0:T(8,128)} %all-gather.3.cloned.1.call-done.f_ref) | copy-start | bytes 6291460
  119.9 197.8 %all-gather.5.cloned.1.call-start = ((), (), s32[]{:S(2)}) async-start(), calls=%async_computation.2 | async-start | bytes 4456448 | tf_op jit(solution)/shard_map/all_gather | solution.py:191
Sparse Core Ops, SparseCore 0:
  69.2 46.0 all-gather.2
  120.0 149.5 all-reduce.1
  271.7 45.9 all-gather.4

commit v2 on v1

--- a/solution.py
+++ b/solution.py
@@ -76,14 +76,20 @@
 
 
 def kernel(n_root, v_ref, g_ref, f_ref, o_ref, a_ref, w_ref, whi, wlo, lhi, llo, scol, srow, r_ref, xhi, xlo):
+    def block(i, j):
+        d = i - j
+        if d <= 4:
+            return g_ref[2 * i:2 * i + 2, d].reshape(BS, BS)
+        return g_ref[2 * j:2 * j + 2, NB - d].reshape(BS, BS).T
+
     eye = lax.broadcasted_iota(jnp.int32, (BS, BS), 0) == lax.broadcasted_iota(jnp.int32, (BS, BS), 1)
     for k in range(NB):
-        d = jnp.where(eye, g_ref[k * BS:(k + 1) * BS, k * BS:(k + 1) * BS], 0.0)
+        d = jnp.where(eye, block(k, k), 0.0)
         srow[:, k * BS:(k + 1) * BS] = jnp.broadcast_to(lax.rsqrt(jnp.sum(d, axis=0, keepdims=True)), (8, BS))
         scol[k * BS:(k + 1) * BS, :] = jnp.broadcast_to(lax.rsqrt(jnp.sum(d, axis=1, keepdims=True)), (BS, BS))
 
     def column(k):
-        s = g_ref[k * BS:, k * BS:(k + 1) * BS] * scol[k * BS:, :] * srow[0:1, k * BS:(k + 1) * BS]
+        s = jnp.concatenate([block(i, k) for i in range(k, NB)], axis=0) * scol[k * BS:, :] * srow[0:1, k * BS:(k + 1) * BS]
         if k:
             rows = (lhi[k * BS:, :k * BS], llo[k * BS:, :k * BS])
             own = (lhi[k * BS:(k + 1) * BS, :k * BS], llo[k * BS:(k + 1) * BS, :k * BS])
@@ -121,7 +127,7 @@
         h, l = split(cur * srow[0:1, k * BS:(k + 1) * BS])
         xhi[:, k * BS:(k + 1) * BS] = h
         xlo[:, k * BS:(k + 1) * BS] = l
-    o_ref[...] = mm3((xhi[...], xlo[...]), split(f_ref[...]))
+    o_ref[...] = mm3((xhi[...], xlo[...]), split(f_ref[...].reshape(M, 512)))
 
 
 def k2(v, g, f, n_root=128.0):
@@ -140,57 +146,212 @@
         compiler_params=pltpu.CompilerParams(vmem_limit_bytes=48 << 20),
     )(v, g, f)
 
-HB = 3
-STEPS = 4
-
-
-def with_halo(shard, sides, width):
-    for axis, dim in sides:
-        devices, length = (lax.axis_size(axis), shard.shape[dim])
-        up = [(i, (i + 1) % devices) for i in range(devices)]
-        down = [(j, i) for i, j in up]
-        last = lax.slice_in_dim(shard, length - width, length, axis=dim)
-        initial = lax.slice_in_dim(shard, 0, width, axis=dim)
-        before = lax.ppermute(last, axis, up)
-        after = lax.ppermute(initial, axis, down)
-        shard = jnp.concatenate([before, shard, after], axis=dim)
-    return shard
-
-
-def operate(field, band):
-    extended = with_halo(field, (("rows", 1),), HB * BS)
-    parts = [
-        jnp.einsum("mj,ji->mi", extended[:, b * BS:(b + 2 * HB + 1) * BS], band[b], precision=lax.Precision.HIGHEST)
-        for b in range(band.shape[0])
-    ]
-    return jnp.concatenate(parts, axis=1)
+
+MESH = pl.DeviceIdType.MESH
+NR, NY, ND, NQ = 32, 8, 5, 20
+HALO, W = 384, 512
+
+
+def device_of(q):
+    return (q * 8) // 5
+
+
+def k1_kernel(columns_ref, tiles_ref, y0_ref, f_out, g_out, wt, ys, hl, hr, gath, gb, part, inbox,
+              hs, hrl, hrr, fs, fr, gs, gr, ds, dr, es, er, out_sem):
+    r, v = lax.axis_index("rows"), lax.axis_index("vecs")
+    y, c = v // 2, v % 2
+    sib, yr, yl = y * 2 + 1 - c, lax.rem(y + 1, NY) * 2 + c, lax.rem(y + NY - 1, NY) * 2 + c
+    right, left = lax.rem(r + 1, NR), lax.rem(r + NR - 1, NR)
+
+    barrier = pltpu.get_barrier_semaphore()
+
+    def greet(d, _):
+        pl.semaphore_signal(barrier, inc=1, device_id=(lax.rem(r + d, NR), v), device_id_type=MESH)
+        return 0
+    lax.fori_loop(1, NR, greet, 0)
+    for other in (sib, yr, yl):
+        pl.semaphore_signal(barrier, inc=1, device_id=(r, other), device_id_type=MESH)
+
+    def rcopy(src, dst, send, recv, to):
+        return pltpu.make_async_remote_copy(src_ref=src, dst_ref=dst, send_sem=send, recv_sem=recv, device_id=to, device_id_type=MESH)
+
+    wt[...] = jnp.zeros_like(wt)
+    for b in range(4):
+        rows = slice(b * BS, (b + 1) * BS)
+        for t, o in ((0, 0), (1, -1), (2, 1)):
+            wt[rows, (b + 3 + o) * BS:(b + 4 + o) * BS] = tiles_ref[b, t]
+        for o in (-3, -2, 2, 3):
+            want = lax.rem(r * 4 + b + o + 4 * NR, 4 * NR)
+            tile = jnp.zeros((BS, BS), bf16)
+            for t in (3, 4, 5):
+                tile = jnp.where(columns_ref[b, t] == want, tiles_ref[b, t], tile)
+            wt[rows, (b + 3 + o) * BS:(b + 4 + o) * BS] = tile
+
+    pl.semaphore_wait(barrier, NR - 1 + 3)
+
+    def stacked(x):
+        return jnp.concatenate(split(x), axis=0)
+
+    def halves(x):
+        return x[:64] + x[64:]
+
+    waits = []
+    for s in range(4):
+        src = y0_ref if s == 0 else ys.at[s - 1]
+        to_right = rcopy(src.at[:, W - HALO:], hl.at[s], hs.at[2 * s], hrl.at[s], (right, v))
+        to_left = rcopy(src.at[:, :HALO], hr.at[s], hs.at[2 * s + 1], hrr.at[s], (left, v))
+        to_right.start()
+        to_left.start()
+        waits += [to_right, to_left]
+        cur = src[...]
+        acc = halves(mm(stacked(cur), wt[:, HALO:HALO + W], True))
+        if s == 1:
+            prev = y0_ref[...]
+        elif s > 1:
+            prev = ys[s - 2]
+        to_right.wait_recv()
+        wl = halves(mm(stacked(hl[s]), wt[:HALO, :HALO], True))
+        to_left.wait_recv()
+        wr = halves(mm(stacked(hr[s]), wt[BS:, HALO + W:], True))
+        parts = [acc[:, :BS] + wl[:, :BS], acc[:, BS:HALO] + wl[:, BS:] + wr[:, :2 * BS], acc[:, HALO:] + wr[:, 2 * BS:]]
+        new = jnp.concatenate(parts, axis=1)
+        if s:
+            new = 2.0 * new - prev
+        if s < 3:
+            ys[s] = new
+        else:
+            gath[v] = new
+
+    def ring(buf, cut, send, recv, each):
+        def slot(d):
+            return lax.rem(y + NY + d, NY) * 2 + c
+
+        def other(d):
+            return lax.rem(y + NY + d, NY) * 2 + 1 - c
+
+        def block(i, part=None):
+            return buf.at[i] if part is None else buf.at[i, part]
+        lo, hi = pl.ds(0, cut), pl.ds(cut, cut)
+
+        def go(i, n, to, part=None):
+            k = rcopy(block(i, part), block(i, part), send.at[n], recv.at[n], (r, to))
+            k.start()
+            waits.append(k)
+
+        def arrive(i, n, part=None):
+            rcopy(block(i, part), block(i, part), send.at[n], recv.at[n], (r, sib)).wait_recv()
+        go(v, 0, yr)
+        go(v, 4, yl)
+        go(v, 11, sib)
+        for s in range(1, 4):
+            p, q = (lo, hi) if s == 3 else (None, None)
+            arrive(slot(-s), s - 1)
+            go(slot(-s), s, yr, p)
+            go(slot(-s), 11 - s, sib)
+            arrive(slot(s), 3 + s)
+            go(slot(s), 4 + s, yl, q)
+            go(slot(s), 11 + s, sib)
+            if s == 1:
+                arrive(other(0), 11)
+            else:
+                arrive(other(1 - s), 12 - s)
+            each(1 - s)
+        arrive(other(-3), 8)
+        each(-3)
+        arrive(slot(4), 3, lo)
+        go(slot(4), 15, sib, lo)
+        arrive(slot(4), 7, hi)
+        go(slot(4), 16, sib, hi)
+        arrive(other(4), 15, lo)
+        arrive(other(4), 16, hi)
+        each(-4)
+        for d in (1, 2, 3):
+            arrive(other(d), 11 + d)
+
+    own = split(gath[v])
+
+    def gram_part(d):
+        at = lax.rem(y + NY + d, NY)
+        pair = split(gath[pl.ds(at * 2, 2)].reshape(BS, W))
+        g = mm3(own, pair, True)
+        for t in range(4):
+            q = -d * 4 + t
+            part[q] = g[t * 16:(t + 1) * 16]
+            to = device_of(q)
+            rel = lax.rem(r - to + NR, NR)
+
+            @pl.when(r != to)
+            def _():
+                rcopy(part.at[q], inbox.at[rel], ds.at[q], dr.at[rel], (to, v)).start()
+
+    ring(gath, 32, fs, fr, gram_part)
+    f_copy = pltpu.make_async_copy(gath, f_out, out_sem.at[0])
+    f_copy.start()
+
+    z = r % 8
+    zq = (z * 5 + 4) // 8
+    mine = (r // 8) * 5 + zq
+    active = (zq * 8) // 5 == z
+
+    @pl.when(active)
+    def _():
+        def add(rel, total):
+            rcopy(part.at[0], inbox.at[rel], ds.at[0], dr.at[rel], (right, v)).wait_recv()
+            return total + inbox[rel]
+        gb[v, mine] = lax.fori_loop(1, NR, add, part[mine])
+
+        def send(rel, _):
+            rcopy(gb.at[v, mine], gb.at[v, mine], es.at[rel], er.at[mine], (lax.rem(r + rel, NR), v)).start()
+            return 0
+        lax.fori_loop(1, NR, send, 0)
+    for q in range(NQ):
+        @pl.when(r != device_of(q))
+        def _():
+            rcopy(gb.at[v, q], gb.at[v, q], es.at[0], er.at[q], (right, v)).wait_recv()
+
+    ring(gb, NQ // 2, gs, gr, lambda d: None)
+    g_copy = pltpu.make_async_copy(gb, g_out, out_sem.at[1])
+    g_copy.start()
+    for k in waits:
+        k.wait_send()
+    for q in range(NQ):
+        @pl.when(r != device_of(q))
+        def _():
+            rcopy(part.at[q], inbox.at[0], ds.at[q], dr.at[0], (right, v)).wait_send()
+
+    @pl.when(active)
+    def _():
+        def done(rel, _):
+            rcopy(gb.at[v, mine], gb.at[v, mine], es.at[rel], er.at[mine], (right, v)).wait_send()
+            return 0
+        lax.fori_loop(1, NR, done, 0)
+    f_copy.wait()
+    g_copy.wait()
+
+
+def k1(tiles, columns, start):
+    vm = pl.BlockSpec(memory_space=pltpu.VMEM)
+    dma = pltpu.SemaphoreType.DMA
+    return pl.pallas_call(
+        k1_kernel,
+        out_shape=(jax.ShapeDtypeStruct((16, 64, W), f32), jax.ShapeDtypeStruct((16, NQ, 16, BS), f32)),
+        in_specs=[pl.BlockSpec(memory_space=pltpu.SMEM), vm, vm],
+        out_specs=(pl.BlockSpec(memory_space=pl.ANY), pl.BlockSpec(memory_space=pl.ANY)),
+        scratch_shapes=[
+            pltpu.VMEM((W, W + 2 * HALO), bf16), pltpu.VMEM((3, 64, W), f32),
+            pltpu.VMEM((4, 64, HALO), f32), pltpu.VMEM((4, 64, HALO), f32),
+            pltpu.VMEM((16, 64, W), f32), pltpu.VMEM((16, NQ, 16, BS), f32),
+            pltpu.VMEM((NQ, 16, BS), f32), pltpu.VMEM((NR, 16, BS), f32),
+            dma((8,)), dma((4,)), dma((4,)), dma((17,)), dma((17,)), dma((17,)), dma((17,)),
+            dma((NQ,)), dma((NR,)), dma((NR,)), dma((NQ,)), dma((2,))],
+        compiler_params=pltpu.CompilerParams(collective_id=0, has_side_effects=True, vmem_limit_bytes=32 << 20),
+    )(columns, tiles, start)
 
 
 def body(tiles, columns, start_vectors):
-    blocks_here = tiles.shape[0]
-    total_blocks = blocks_here * lax.axis_size("rows")
-    first_block = lax.axis_index("rows") * blocks_here
-    global_rows = first_block + jnp.arange(blocks_here, dtype=jnp.int32)
-    offsets = jnp.mod(columns - global_rows[:, None] + HB, total_blocks)
-    chosen = offsets[:, None, :] == jnp.arange(2 * HB + 1, dtype=jnp.int32)[None, :, None]
-    tiles32 = jnp.swapaxes(tiles.astype(jnp.float32), 2, 3)
-    band = jnp.zeros((blocks_here, 2 * HB + 1, BS, BS), jnp.float32)
-    for t in range(tiles.shape[1]):
-        band = band + jnp.where(chosen[:, :, t, None, None], tiles32[:, None, t], 0.0)
-    band = band.reshape(blocks_here, (2 * HB + 1) * BS, BS)
-    previous = start_vectors
-    current = operate(start_vectors, band)
-    for step in range(STEPS - 1):
-        following = 2.0 * operate(current, band) - previous
-        previous = current
-        current = following
-    width = current.shape[0]
-    gathered = lax.all_gather(current, "vecs", axis=0, tiled=True)
-    partial_rows = jnp.einsum("mn,kn->mk", current, gathered, precision=lax.Precision.HIGHEST)
-    summed_rows = lax.psum(partial_rows, "rows")
-    gram = lax.all_gather(summed_rows, "vecs", axis=0, tiled=True)
+    gathered, gram = k1(tiles, columns, start_vectors)
     where = lax.axis_index("vecs").astype(jnp.int32).reshape(1)
-    return k2(where, gram, gathered)
+    return k2(where, gram.reshape(16, ND, 64, BS), gathered)
 
 
 def solution(mesh):

time: 365 us -> 133 us (0.36)
  waiting for transfers between devices: 251 us -> 0 us
  Pallas kernels: 40.3 us -> 130 us
  starting transfers between devices: 42.4 us -> 0 us
  between operations: 13.4 us -> 0.01 us
  matrix products: 11.3 us -> 0 us
  other arithmetic: 3.78 us -> 0 us
    psum x1 -> x0, waiting for transfers between devices: 149 us -> none  [body(): summed_rows = lax.psum(partial_rows, 'rows')]
    all_gather x2 -> x0, waiting for transfers between devices: 94.3 us -> none  [the longest x1 48.1 us: body(): gram = lax.all_gather(summed_rows, 'vecs', axis=0, tiled=True)]
    pallas_call x0 -> x1, Pallas kernels: none -> 92.2 us  [k1(): pl.pallas_call(k1_kernel, out_shape=(jax.ShapeDtypeStruct((16, 64, W), f3...]
    ppermute x8 -> x0, starting transfers between devices: 42.2 us -> none  [the longest x4 34.5 us: with_halo(): after = lax.ppermute(initial, axis, down)]
    dot_general x17 -> x0, matrix products: 11.3 us -> none  [the longest x16 6.7 us: operate(): jnp.einsum('mj,ji->mi', extended[:, b * BS:(b + 2 * HB + 1) * BS], band[b...]
    ppermute x8 -> x0, waiting for transfers between devices: 7.19 us -> none  [the longest x4 4.58 us: with_halo(): after = lax.ppermute(initial, axis, down)]
  transfers between devices with their start and end apart: 11 -> 0, of which waited for: 10 -> 0; matrix products, arithmetic and copies ran while one was open for 1% -> 0% of each run, Pallas kernels for 0% -> 0%
where the time goes in v2:
time: 133 us
  Pallas kernels  130 us (98%)
  local copies, waits for them, and re-layouts  2.72 us (2%)
    pallas_call x1, Pallas kernels, k1(): pl.pallas_call(k1_kernel, out_shape=(jax.ShapeDtypeStruct((16, 64, W), f3...  92.2 us
    pallas_call x1, Pallas kernels, k2(): pl.pallas_call(functools.partial(kernel, n_root), out_shape=jax.ShapeDtyp...  38.2 us
    unnamed x6, local copies, waits for them, and re-layouts  2.72 us

profile of v2, /device:TPU:1, one launch (start us, length us, event | category | flops | bytes accessed | tf_op | source)
XLA Modules:
  0.0 133.1 jit_solution(15022799766086040972)
XLA Ops:
  0.0 0.0 copy-start
  0.0 1.1 copy-done
  1.1 0.0 copy-start.1
  1.1 0.9 copy-done.1
  2.0 0.0 copy-start.2
  2.0 0.7 copy-done.2
  2.7 92.2 %shard_map.37 = (f32[16,64,512]{2,1,0:T(8,128)S(1)}, f32[16,20,16,128]{3,2,1,0:T(8,128)S(1)}) custom-call(s32[4,6]{1,0:T(4,128)S(1)} %copy-done.2, bf16[4,6,128,128]{3,2,1,0:T(8,128)(2,1)S(1)} %copy-done, f32[64,512]{1,0:T(8,128)S(1)} %copy-done.1), custom_call_target="tpu_custom_call" | custom-call | tf_op jit(solution)/shard_map/pallas_call | solution.py:335
  94.9 38.2 %shard_map.38 = f32[64,512]{1,0:T(8,128)} custom-call(s32[1]{0:T(128)} %bitcast.v_ref, f32[16,5,64,128]{3,2,1,0:T(8,128)S(1)} %bitcast.2, f32[16,64,512]{2,1,0:T(8,128)S(1)} %get-tuple-element.8.f_ref), custom_call_target="tpu_custom_call" | custom-call | tf_op jit(solution)/shard_map/pallas_call | solution.py:135
Async XLA Ops:
  0.0 1.1 copy-start
  1.1 0.9 copy-start.1
  2.0 0.7 copy-start.2

commit v3 on v1

v3 whole, which is shorter than its diff:
```python
import functools

import jax
import jax.numpy as jnp
from jax import lax
from jax.experimental import pallas as pl
from jax.experimental.pallas import tpu as pltpu
from jax.sharding import PartitionSpec as P

f32, bf16 = jnp.float32, jnp.bfloat16
M, BS, NB, GR = 1024, 128, 8, 8
MESH = pl.DeviceIdType.MESH
NR, NY, ND, NQ = 32, 8, 5, 20
HALO, W, HALF = 384, 512, 32


def split(x):
    hi = x.astype(bf16)
    return hi, (x - hi.astype(f32)).astype(bf16)


def mm(a, b, tb):
    dims = (((1,), (1 if tb else 0,)), ((), ()))
    return lax.dot_general(a, b, dims, preferred_element_type=f32)


def mm3(a, b, tb=False):
    return mm(a[0], b[0], tb) + (mm(a[0], b[1], tb) + mm(a[1], b[0], tb))


def recip(x):
    r = pl.reciprocal(x, approx=True)
    return r * (2.0 - x * r)


def diag_factor(a_ref, w_ref, srow_ref):
    full = a_ref[:BS, :]
    eye = lax.broadcasted_iota(jnp.int32, (BS, BS), 0) == lax.broadcasted_iota(jnp.int32, (BS, BS), 1)
    only = jnp.where(eye, full, 0.0)
    srow = lax.rsqrt(jnp.sum(only, axis=0, keepdims=True))
    srow_ref[...] = jnp.broadcast_to(srow, (8, BS))
    a_ref[:BS, :] = full * srow * lax.rsqrt(jnp.sum(only, axis=1, keepdims=True))
    lane = lax.broadcasted_iota(jnp.int32, (8, BS), 1)
    sub = lax.broadcasted_iota(jnp.int32, (8, BS), 0)
    for g in range(BS // GR):
        lo = g * GR
        ing = (lane >= lo) & (lane < lo + GR)
        p = a_ref[lo:lo + 8, :]
        cols = [jnp.broadcast_to(p[:, lo + j:lo + j + 1], (8, BS)) for j in range(GR)]
        x = jnp.where(lane == sub + lo, 1.0, jnp.where(ing, 0.0, p))
        w = x
        for j in range(0, GR, 2):
            cj, ck = cols[j], cols[j + 1]

            def row(v, i):
                return jnp.broadcast_to(v[i:i + 1, :], (8, BS))
            a, b, c = row(cj, j), row(cj, j + 1), row(ck, j + 1)
            det = a * c - b * b
            pair = (sub == j) | (sub == j + 1)
            cjm = jnp.where(sub == j, -1.0, jnp.where(sub == j + 1, 0.0, cj))
            ckm = jnp.where(sub == j + 1, -1.0, jnp.where(sub == j, 0.0, ck))
            r = recip(det)
            x0, x1 = row(x, j), row(x, j + 1)
            y1 = a * x1 - b * x0
            w = jnp.where(sub == j, x0 * lax.rsqrt(a), jnp.where(sub == j + 1, y1 * lax.rsqrt(a * det), w))
            for m in list(range(j + 2, GR)) + [-1]:
                v = x if m < 0 else cols[m]
                v0, v1 = row(v, j), row(v, j + 1)
                y0 = c * v0 - b * v1
                y1 = a * v1 - b * v0
                z = cjm * y0 + ckm * y1
                new = jnp.where(pair, 0.0, v) - r * z
                if m < 0:
                    x = new
                else:
                    cols[m] = new
        w_ref[lo:lo + 8, :] = jnp.where(lane < lo + GR, w, 0.0)
        for h in range(g + 1, BS // GR):
            q = a_ref[h * 8:h * 8 + 8, :]
            cs = [jnp.broadcast_to(q[:, lo + j:lo + j + 1], (8, BS)) for j in range(GR)]
            t = [cs[j] * jnp.broadcast_to(x[j:j + 1, :], (8, BS)) for j in range(GR)]
            while len(t) > 1:
                t = [t[i] + t[i + 1] for i in range(0, len(t), 2)]
            a_ref[h * 8:h * 8 + 8, :] = jnp.where(ing, 0.0, q) - t[0]


def device_of(q):
    return (q * 8) // 5


def transfers(k):
    return [(i, i - k) for i in range(k, min(k + 5, NB))] + [(k, d) for d in range(k + 1, 4)]


def kernel(n_root, columns_ref, tiles_ref, y0_ref, o_ref, wt, ys, hl, hr, gath, gb, part, inbox,
           a_ref, w_ref, srow, whi, wlo, lhi, llo, r_ref, xhi, xlo,
           hs, hrl, hrr, fs, fr, ds, dr, es, er, ts, tr, tf, tb):
    r, v = lax.axis_index("rows"), lax.axis_index("vecs")
    y, c = v // 2, v % 2
    sib, yr, yl = y * 2 + 1 - c, lax.rem(y + 1, NY) * 2 + c, lax.rem(y + NY - 1, NY) * 2 + c
    right, left = lax.rem(r + 1, NR), lax.rem(r + NR - 1, NR)

    barrier = pltpu.get_barrier_semaphore()

    def greet(d, _):
        pl.semaphore_signal(barrier, inc=1, device_id=(lax.rem(r + d, NR), v), device_id_type=MESH)
        return 0
    lax.fori_loop(1, NR, greet, 0)

    def greet_y(d, _):
        pl.semaphore_signal(barrier, inc=1, device_id=(r, lax.rem(y + d, NY) * 2 + c), device_id_type=MESH)
        return 0
    lax.fori_loop(1, NY, greet_y, 0)
    pl.semaphore_signal(barrier, inc=1, device_id=(r, sib), device_id_type=MESH)

    def rcopy(src, dst, send, recv, to):
        return pltpu.make_async_remote_copy(src_ref=src, dst_ref=dst, send_sem=send, recv_sem=recv, device_id=to, device_id_type=MESH)

    wt[...] = jnp.zeros_like(wt)
    for b in range(4):
        rows = slice(b * BS, (b + 1) * BS)
        for t, o in ((0, 0), (1, -1), (2, 1)):
            wt[rows, (b + 3 + o) * BS:(b + 4 + o) * BS] = tiles_ref[b, t]
        for o in (-3, -2, 2, 3):
            want = lax.rem(r * 4 + b + o + 4 * NR, 4 * NR)
            tile = jnp.zeros((BS, BS), bf16)
            for t in (3, 4, 5):
                tile = jnp.where(columns_ref[b, t] == want, tiles_ref[b, t], tile)
            wt[rows, (b + 3 + o) * BS:(b + 4 + o) * BS] = tile

    pl.semaphore_wait(barrier, NR - 1 + NY - 1 + 1)

    def stacked(x):
        return jnp.concatenate(split(x), axis=0)

    def halves(x):
        n = x.shape[0] // 2
        return x[:n] + x[n:]

    waits = []
    rows_of = (slice(0, HALF), slice(HALF, 2 * HALF))

    def field(s):
        return y0_ref if s == 0 else ys.at[s - 1]

    def halo(s, h, go):
        src, n = field(s), 2 * s + h
        to_right = rcopy(src.at[rows_of[h], W - HALO:], hl.at[s, rows_of[h]], hs.at[2 * n], hrl.at[n], (right, v))
        to_left = rcopy(src.at[rows_of[h], :HALO], hr.at[s, rows_of[h]], hs.at[2 * n + 1], hrr.at[n], (left, v))
        if go:
            to_right.start()
            to_left.start()
            waits.extend((to_right, to_left))
        else:
            to_right.wait_recv()
            to_left.wait_recv()

    def slot(d):
        return lax.rem(y + NY + d, NY) * 2 + c

    def other(d):
        return lax.rem(y + NY + d, NY) * 2 + 1 - c

    def half(i, h):
        return gath.at[i, rows_of[h]]

    def go(i, n, h, to):
        k = rcopy(half(i, h), half(i, h), fs.at[2 * n + h], fr.at[2 * n + h], (r, to))
        k.start()
        waits.append(k)

    def arrive(i, n, h):
        rcopy(half(i, h), half(i, h), fs.at[2 * n + h], fr.at[2 * n + h], (r, sib)).wait_recv()

    halo(0, 0, True)
    halo(0, 1, True)
    for s in range(4):
        acc = halves(mm(stacked(field(s)[...]), wt[:, HALO:HALO + W], True))
        for h in range(2):
            rows = rows_of[h]
            halo(s, h, False)
            wl = halves(mm(stacked(hl[s, rows]), wt[:HALO, :HALO], True))
            wr = halves(mm(stacked(hr[s, rows]), wt[BS:, HALO + W:], True))
            mid = acc[rows]
            parts = [mid[:, :BS] + wl[:, :BS], mid[:, BS:HALO] + wl[:, BS:] + wr[:, :2 * BS], mid[:, HALO:] + wr[:, 2 * BS:]]
            new = jnp.concatenate(parts, axis=1)
            if s:
                new = 2.0 * new - field(s - 1)[rows]
            if s < 3:
                ys[s, rows] = new
                halo(s + 1, h, True)
            else:
                gath[v, rows] = new
                go(v, 0, h, yr)
                go(v, 4, h, yl)
                go(v, 11, h, sib)

    own = split(gath[v])

    def gram_part(d):
        at = lax.rem(y + NY - d, NY)
        pair = split(gath[pl.ds(at * 2, 2)].reshape(BS, W))
        g = mm3(own, pair, True)
        for t in range(4):
            q = d * 4 + t
            part[q] = g[t * 16:(t + 1) * 16]
            to = device_of(q)
            rel = lax.rem(r - to + NR, NR)

            @pl.when(r != to)
            def _():
                rcopy(part.at[q], inbox.at[rel], ds.at[q], dr.at[rel], (to, v)).start()

    for s in range(1, 4):
        for h in range(2):
            arrive(slot(-s), s - 1, h)
            if s < 3 or h == 0:
                go(slot(-s), s, h, yr)
            go(slot(-s), 11 - s, h, sib)
            arrive(slot(s), 3 + s, h)
            if s < 3 or h == 1:
                go(slot(s), 4 + s, h, yl)
            go(slot(s), 11 + s, h, sib)
        for h in range(2):
            arrive(other(1 - s), 12 - s, h)
        gram_part(s - 1)
    for h in range(2):
        arrive(other(-3), 8, h)
    gram_part(3)
    arrive(slot(4), 3, 0)
    go(slot(4), 15, 0, sib)
    arrive(slot(4), 7, 1)
    go(slot(4), 15, 1, sib)
    arrive(other(4), 15, 0)
    arrive(other(4), 15, 1)
    gram_part(4)

    z = r % 8
    zq = (z * 5 + 4) // 8
    mine = (r // 8) * 5 + zq
    active = (zq * 8) // 5 == z

    @pl.when(active)
    def _():
        def add(rel, total):
            rcopy(part.at[0], inbox.at[rel], ds.at[0], dr.at[rel], (right, v)).wait_recv()
            return total + inbox[rel]
        gb[v, mine] = lax.fori_loop(1, NR, add, part[mine])

        def send(rel, _):
            rcopy(gb.at[v, mine], gb.at[v, mine], es.at[rel], er.at[mine], (lax.rem(r + rel, NR), v)).start()
            return 0
        lax.fori_loop(1, NR, send, 0)
    for q in range(NQ):
        @pl.when(r != device_of(q))
        def _():
            rcopy(gb.at[v, q], gb.at[v, q], es.at[0], er.at[q], (right, v)).wait_recv()

    def piece(i, d, core):
        return gb.at[i * 2 + core, 4 * d:4 * d + 4]

    def send_block(i, d):
        @pl.when(y == i)
        def _():
            rcopy(piece(i, d, c), piece(i, d, c), ts.at[8 * d], tb.at[5 * i + d], (r, sib)).start()

            def one(n, _):
                rcopy(piece(i, d, c), piece(i, d, c), ts.at[8 * d + n], tr.at[5 * i + d], (r, lax.rem(y + n, NY) * 2 + c)).start()
                return 0
            lax.fori_loop(1, NY, one, 0)

    def pass_block(i, d):
        @pl.when(y != i)
        def _():
            rcopy(piece(i, d, c), piece(i, d, c), ts.at[0], tr.at[5 * i + d], (r, sib)).wait_recv()
            rcopy(piece(i, d, c), piece(i, d, c), tf.at[5 * i + d], tb.at[5 * i + d], (r, sib)).start()

    def take_block(i, d):
        rcopy(piece(i, d, 1 - c), piece(i, d, 1 - c), ts.at[0], tb.at[5 * i + d], (r, sib)).wait_recv()

    def block(i, j):
        d = i - j
        if d <= 4:
            return gb[2 * i:2 * i + 2, 4 * d:4 * d + 4].reshape(BS, BS)
        d = NB - d
        return gb[2 * j:2 * j + 2, 4 * d:4 * d + 4].reshape(BS, BS).T

    def column(k):
        s = jnp.concatenate([block(i, k) for i in range(k, NB)], axis=0)
        if k:
            rows = (lhi[k * BS:, :k * BS], llo[k * BS:, :k * BS])
            own = (lhi[k * BS:(k + 1) * BS, :k * BS], llo[k * BS:(k + 1) * BS, :k * BS])
            s = s - mm3(rows, own, True)
        return s

    for i, d in transfers(0) + transfers(1):
        send_block(i, d)
    pass_block(0, 0)
    take_block(0, 0)
    a_ref[:BS, :] = block(0, 0)

    def after(k):
        hi, lo = split(w_ref[...] * srow[0:1, :])
        whi[k], wlo[k] = hi, lo
        if k + 1 == NB:
            return
        if k + 2 < NB:
            for i, d in transfers(k + 2):
                send_block(i, d)
        todo = (transfers(0)[1:] if k == 0 else []) + transfers(k + 1)
        for i, d in todo:
            pass_block(i, d)
        for i, d in todo:
            take_block(i, d)
        if k == 0:
            a_ref[BS:, :] = column(0)[BS:]
        h, l = split(mm3(split(a_ref[BS:M - k * BS, :]), (hi, lo), True))
        lhi[(k + 1) * BS:, k * BS:(k + 1) * BS] = h
        llo[(k + 1) * BS:, k * BS:(k + 1) * BS] = l
        a_ref[0:M - (k + 1) * BS, :] = column(k + 1)

    def step(k, _):
        diag_factor(a_ref, w_ref, srow)
        for kk in range(NB):
            @pl.when(k == kk)
            def _():
                after(kk)
        return 0
    lax.fori_loop(0, NB, step, 0)

    sel = lax.broadcasted_iota(jnp.int32, (64, M), 0) + v * 64 == lax.broadcasted_iota(jnp.int32, (64, M), 1)
    r_ref[...] = jnp.where(sel, f32(n_root), 0.0)
    for k in range(NB - 1, -1, -1):
        x = split(mm3(split(r_ref[:, k * BS:(k + 1) * BS]), (whi[k], wlo[k])))
        if k:
            r_ref[:, :k * BS] -= mm3(x, (lhi[k * BS:(k + 1) * BS, :k * BS], llo[k * BS:(k + 1) * BS, :k * BS]))
        xhi[:, k * BS:(k + 1) * BS] = x[0]
        xlo[:, k * BS:(k + 1) * BS] = x[1]
    for d in (1, 2, 3):
        for h in range(2):
            arrive(other(d), 11 + d, h)
    o_ref[...] = mm3((xhi[...], xlo[...]), split(gath[...].reshape(M, W)))

    for k in waits:
        k.wait_send()
    for q in range(NQ):
        @pl.when(r != device_of(q))
        def _():
            rcopy(part.at[q], inbox.at[0], ds.at[q], dr.at[0], (right, v)).wait_send()

    @pl.when(active)
    def _():
        def done(rel, _):
            rcopy(gb.at[v, mine], gb.at[v, mine], es.at[rel], er.at[mine], (right, v)).wait_send()
            return 0
        lax.fori_loop(1, NR, done, 0)

    def sent(n, _):
        rcopy(piece(0, 0, c), piece(0, 0, c), ts.at[n], tr.at[0], (r, sib)).wait_send()
        return 0
    lax.fori_loop(0, 32, sent, 0)

    @pl.when(y >= 4)
    def _():
        lax.fori_loop(32, 40, sent, 0)
    for k in range(NB):
        for i, d in transfers(k):
            @pl.when(y != i)
            def _():
                rcopy(piece(i, d, c), piece(i, d, c), tf.at[5 * i + d], tb.at[5 * i + d], (r, sib)).wait_send()


def solve(tiles, columns, start, n_root=128.0):
    vm = pl.BlockSpec(memory_space=pltpu.VMEM)
    dma = pltpu.SemaphoreType.DMA
    return pl.pallas_call(
        functools.partial(kernel, n_root),
        out_shape=jax.ShapeDtypeStruct((64, W), f32),
        in_specs=[pl.BlockSpec(memory_space=pltpu.SMEM), vm, vm],
        out_specs=vm,
        scratch_shapes=[
            pltpu.VMEM((W, W + 2 * HALO), bf16), pltpu.VMEM((3, 64, W), f32),
            pltpu.VMEM((4, 64, HALO), f32), pltpu.VMEM((4, 64, HALO), f32),
            pltpu.VMEM((16, 64, W), f32), pltpu.VMEM((16, NQ, 16, BS), f32),
            pltpu.VMEM((NQ, 16, BS), f32), pltpu.VMEM((NR, 16, BS), f32),
            pltpu.VMEM((M, BS), f32), pltpu.VMEM((BS, BS), f32), pltpu.VMEM((8, BS), f32),
            pltpu.VMEM((NB, BS, BS), bf16), pltpu.VMEM((NB, BS, BS), bf16),
            pltpu.VMEM((M, M), bf16), pltpu.VMEM((M, M), bf16),
            pltpu.VMEM((64, M), f32), pltpu.VMEM((64, M), bf16), pltpu.VMEM((64, M), bf16),
            dma((16,)), dma((8,)), dma((8,)), dma((32,)), dma((32,)),
            dma((NQ,)), dma((NR,)), dma((NR,)), dma((NQ,)),
            dma((40,)), dma((40,)), dma((40,)), dma((40,))],
        compiler_params=pltpu.CompilerParams(collective_id=0, has_side_effects=True, vmem_limit_bytes=48 << 20),
    )(columns, tiles, start)


def solution(mesh):
    placed = (P("rows", None, None, None), P("rows", None), P("vecs", "rows"))
    return jax.shard_map(
        solve, mesh=mesh, in_specs=placed, out_specs=P("vecs", "rows"), check_vma=False
    )
```

time: 365 us -> 142 us (0.39)
  the two profiles are of different devices: /device:TPU:1 before, /device:TPU:18 now
where the time goes in v3:
time: 142 us
  Pallas kernels  139 us (98%)
  local copies, waits for them, and re-layouts  3.38 us (2%)
    pallas_call x1, Pallas kernels, solve(): pl.pallas_call(functools.partial(kernel, n_root), out_shape=jax.ShapeDtyp...  139 us
    unnamed x7, local copies, waits for them, and re-layouts  3.38 us

profile of v3, /device:TPU:18, one launch (start us, length us, event | category | flops | bytes accessed | tf_op | source)
XLA Modules:
  0.0 142.1 jit_solution(3361729146938167779)
XLA Ops:
  0.0 0.0 copy-start
  0.0 1.1 copy-done
  1.1 0.0 copy-start.1
  1.1 0.9 copy-done.1
  2.0 0.0 copy-start.2
  2.0 0.7 copy-done.2
  2.7 138.7 %shard_map.37 = f32[64,512]{1,0:T(8,128)S(1)} custom-call(s32[4,6]{1,0:T(4,128)S(1)} %copy-done.2, bf16[4,6,128,128]{3,2,1,0:T(8,128)(2,1)S(1)} %copy-done, f32[64,512]{1,0:T(8,128)S(1)} %copy-done.1), custom_call_target="tpu_custom_call" | custom-call | tf_op jit(solution)/shard_map/pallas_call | solution.py:376
  141.4 0.7 copy.5
Async XLA Ops:
  0.0 1.1 copy-start
  1.1 0.9 copy-start.1
  2.0 0.7 copy-start.2

commit v4 on v3

--- a/solution.py
+++ b/solution.py
@@ -1,4 +1,5 @@
 import functools
+import types
 
 import jax
 import jax.numpy as jnp
@@ -88,13 +89,15 @@
     return (q * 8) // 5
 
 
-def transfers(k):
-    return [(i, i - k) for i in range(k, min(k + 5, NB))] + [(k, d) for d in range(k + 1, 4)]
-
-
-def kernel(n_root, columns_ref, tiles_ref, y0_ref, o_ref, wt, ys, hl, hr, gath, gb, part, inbox,
+EARLY = ((0, 0), (1, 0), (1, 1))
+
+
+def kernel(n_root, columns_ref, tiles_in, y0_in, o_ref, tiles_ref, y0_ref, wt, ys, hl, hr, gath, gb, ub, part, inbox,
            a_ref, w_ref, srow, whi, wlo, lhi, llo, r_ref, xhi, xlo,
-           hs, hrl, hrr, fs, fr, ds, dr, es, er, ts, tr, tf, tb):
+           ls, hs, hrl, hrr, fs, fr, gs, gr, ds, dr, es, er, us, ur, uf, ub_sem):
+    loads = [pltpu.make_async_copy(a, b, ls.at[n]) for n, (a, b) in enumerate(((y0_in, y0_ref), (tiles_in, tiles_ref)))]
+    for load in loads:
+        load.start()
     r, v = lax.axis_index("rows"), lax.axis_index("vecs")
     y, c = v // 2, v % 2
     sib, yr, yl = y * 2 + 1 - c, lax.rem(y + 1, NY) * 2 + c, lax.rem(y + NY - 1, NY) * 2 + c
@@ -116,6 +119,8 @@
     def rcopy(src, dst, send, recv, to):
         return pltpu.make_async_remote_copy(src_ref=src, dst_ref=dst, send_sem=send, recv_sem=recv, device_id=to, device_id_type=MESH)
 
+    for load in loads:
+        load.wait()
     wt[...] = jnp.zeros_like(wt)
     for b in range(4):
         rows = slice(b * BS, (b + 1) * BS)
@@ -155,22 +160,55 @@
             to_right.wait_recv()
             to_left.wait_recv()
 
-    def slot(d):
-        return lax.rem(y + NY + d, NY) * 2 + c
-
-    def other(d):
-        return lax.rem(y + NY + d, NY) * 2 + 1 - c
-
-    def half(i, h):
-        return gath.at[i, rows_of[h]]
-
-    def go(i, n, h, to):
-        k = rcopy(half(i, h), half(i, h), fs.at[2 * n + h], fr.at[2 * n + h], (r, to))
-        k.start()
-        waits.append(k)
-
-    def arrive(i, n, h):
-        rcopy(half(i, h), half(i, h), fs.at[2 * n + h], fr.at[2 * n + h], (r, sib)).wait_recv()
+    def ring(half, send, recv):
+        started = set()
+
+        def slot(d):
+            return lax.rem(y + NY + d, NY) * 2 + c
+
+        def other(d):
+            return lax.rem(y + NY + d, NY) * 2 + 1 - c
+
+        def go(i, n, h, to):
+            rcopy(half(i, h), half(i, h), send.at[2 * n + h], recv.at[2 * n + h], (r, to)).start()
+            started.add((n, h))
+
+        def finish():
+            for n, h in sorted(started):
+                rcopy(half(v, h), half(v, h), send.at[2 * n + h], recv.at[2 * n + h], (r, sib)).wait_send()
+
+        def arrive(i, n, h):
+            rcopy(half(i, h), half(i, h), send.at[2 * n + h], recv.at[2 * n + h], (r, sib)).wait_recv()
+
+        def first(h):
+            go(v, 0, h, yr)
+            go(v, 4, h, yl)
+            go(v, 11, h, sib)
+
+        def hop(s):
+            for h in range(2):
+                arrive(slot(-s), s - 1, h)
+                if s < 3 or h == 0:
+                    go(slot(-s), s, h, yr)
+                go(slot(-s), 11 - s, h, sib)
+                arrive(slot(s), 3 + s, h)
+                if s < 3 or h == 1:
+                    go(slot(s), 4 + s, h, yl)
+                go(slot(s), 11 + s, h, sib)
+
+        def across(d):
+            for h in range(2):
+                arrive(other(d), 15 if d == 4 else 11 + d, h)
+
+        def last():
+            arrive(slot(4), 3, 0)
+            go(slot(4), 15, 0, sib)
+            arrive(slot(4), 7, 1)
+            go(slot(4), 15, 1, sib)
+        return types.SimpleNamespace(first=first, hop=hop, across=across, last=last, finish=finish)
+
+    vectors = ring(lambda i, h: gath.at[i, rows_of[h]], fs, fr)
+    grams = ring(lambda i, h: gb.at[i, 10 * h:10 * h + 10], gs, gr)
 
     halo(0, 0, True)
     halo(0, 1, True)
@@ -191,9 +229,7 @@
                 halo(s + 1, h, True)
             else:
                 gath[v, rows] = new
-                go(v, 0, h, yr)
-                go(v, 4, h, yl)
-                go(v, 11, h, sib)
+                vectors.first(h)
 
     own = split(gath[v])
 
@@ -211,72 +247,81 @@
             def _():
                 rcopy(part.at[q], inbox.at[rel], ds.at[q], dr.at[rel], (to, v)).start()
 
-    for s in range(1, 4):
-        for h in range(2):
-            arrive(slot(-s), s - 1, h)
-            if s < 3 or h == 0:
-                go(slot(-s), s, h, yr)
-            go(slot(-s), 11 - s, h, sib)
-            arrive(slot(s), 3 + s, h)
-            if s < 3 or h == 1:
-                go(slot(s), 4 + s, h, yl)
-            go(slot(s), 11 + s, h, sib)
-        for h in range(2):
-            arrive(other(1 - s), 12 - s, h)
-        gram_part(s - 1)
-    for h in range(2):
-        arrive(other(-3), 8, h)
-    gram_part(3)
-    arrive(slot(4), 3, 0)
-    go(slot(4), 15, 0, sib)
-    arrive(slot(4), 7, 1)
-    go(slot(4), 15, 1, sib)
-    arrive(other(4), 15, 0)
-    arrive(other(4), 15, 1)
-    gram_part(4)
-
     z = r % 8
     zq = (z * 5 + 4) // 8
     mine = (r // 8) * 5 + zq
     active = (zq * 8) // 5 == z
 
-    @pl.when(active)
-    def _():
-        def add(rel, total):
-            rcopy(part.at[0], inbox.at[rel], ds.at[0], dr.at[rel], (right, v)).wait_recv()
-            return total + inbox[rel]
-        gb[v, mine] = lax.fori_loop(1, NR, add, part[mine])
-
-        def send(rel, _):
-            rcopy(gb.at[v, mine], gb.at[v, mine], es.at[rel], er.at[mine], (lax.rem(r + rel, NR), v)).start()
-            return 0
-        lax.fori_loop(1, NR, send, 0)
-    for q in range(NQ):
-        @pl.when(r != device_of(q))
-        def _():
-            rcopy(gb.at[v, q], gb.at[v, q], es.at[0], er.at[q], (right, v)).wait_recv()
-
-    def piece(i, d, core):
-        return gb.at[i * 2 + core, 4 * d:4 * d + 4]
-
-    def send_block(i, d):
+    def share(d):
+        @pl.when(active & (mine // 4 == d))
+        def _():
+            def add(rel, total):
+                rcopy(part.at[0], inbox.at[rel], ds.at[0], dr.at[rel], (right, v)).wait_recv()
+                return total + inbox[rel]
+            gb[v, mine] = lax.fori_loop(1, NR, add, part[mine])
+
+            def send(rel, _):
+                rcopy(gb.at[v, mine], gb.at[v, mine], es.at[rel], er.at[mine], (lax.rem(r + rel, NR), v)).start()
+                return 0
+            lax.fori_loop(1, NR, send, 0)
+
+    def shared(d):
+        for q in range(4 * d, 4 * d + 4):
+            @pl.when(r != device_of(q))
+            def _():
+                rcopy(gb.at[v, q], gb.at[v, q], es.at[0], er.at[q], (right, v)).wait_recv()
+
+    vectors.hop(1)
+    vectors.across(0)
+    gram_part(0)
+    vectors.hop(2)
+    vectors.across(-1)
+    gram_part(1)
+    vectors.hop(3)
+    vectors.across(-2)
+    gram_part(2)
+    share(0)
+    vectors.across(-3)
+    gram_part(3)
+    vectors.last()
+    vectors.across(4)
+    gram_part(4)
+    for d in range(1, ND):
+        share(d)
+    shared(0)
+    shared(1)
+
+    def early(n):
+        i, j = EARLY[n]
+        d = i - j
+        return i, gb.at[v, 4 * d:4 * d + 4], ub.at[n, c]
+
+    for n in range(3):
+        i, src, dst = early(n)
+
         @pl.when(y == i)
         def _():
-            rcopy(piece(i, d, c), piece(i, d, c), ts.at[8 * d], tb.at[5 * i + d], (r, sib)).start()
-
-            def one(n, _):
-                rcopy(piece(i, d, c), piece(i, d, c), ts.at[8 * d + n], tr.at[5 * i + d], (r, lax.rem(y + n, NY) * 2 + c)).start()
+            ub[n, c] = src[...]
+            rcopy(src, dst, us.at[8 * n], ub_sem.at[n], (r, sib)).start()
+
+            def one(m, _):
+                rcopy(src, dst, us.at[8 * n + m], ur.at[n], (r, lax.rem(y + m, NY) * 2 + c)).start()
                 return 0
             lax.fori_loop(1, NY, one, 0)
-
-    def pass_block(i, d):
+    for d in range(2, ND):
+        shared(d)
+    for h in range(2):
+        grams.first(h)
+    for n in range(3):
+        i, src, dst = early(n)
+
         @pl.when(y != i)
         def _():
-            rcopy(piece(i, d, c), piece(i, d, c), ts.at[0], tr.at[5 * i + d], (r, sib)).wait_recv()
-            rcopy(piece(i, d, c), piece(i, d, c), tf.at[5 * i + d], tb.at[5 * i + d], (r, sib)).start()
-
-    def take_block(i, d):
-        rcopy(piece(i, d, 1 - c), piece(i, d, 1 - c), ts.at[0], tb.at[5 * i + d], (r, sib)).wait_recv()
+            rcopy(dst, dst, us.at[0], ur.at[n], (r, sib)).wait_recv()
+            rcopy(dst, dst, uf.at[n], ub_sem.at[n], (r, sib)).start()
+    for n in range(3):
+        dst = ub.at[n, 1 - c]
+        rcopy(dst, dst, us.at[0], ub_sem.at[n], (r, sib)).wait_recv()
 
     def block(i, j):
         d = i - j
@@ -285,39 +330,40 @@
         d = NB - d
         return gb[2 * j:2 * j + 2, 4 * d:4 * d + 4].reshape(BS, BS).T
 
-    def column(k):
-        s = jnp.concatenate([block(i, k) for i in range(k, NB)], axis=0)
+    def column(k, first=0):
+        top = (k + first) * BS
+        s = jnp.concatenate([block(i, k) for i in range(k + first, NB)], axis=0)
         if k:
-            rows = (lhi[k * BS:, :k * BS], llo[k * BS:, :k * BS])
+            rows = (lhi[top:, :k * BS], llo[top:, :k * BS])
             own = (lhi[k * BS:(k + 1) * BS, :k * BS], llo[k * BS:(k + 1) * BS, :k * BS])
             s = s - mm3(rows, own, True)
         return s
 
-    for i, d in transfers(0) + transfers(1):
-        send_block(i, d)
-    pass_block(0, 0)
-    take_block(0, 0)
-    a_ref[:BS, :] = block(0, 0)
+    def panel(k, first, rows):
+        h, l = split(mm3(split(rows), (whi[k], wlo[k]), True))
+        stop = first * BS + rows.shape[0]
+        lhi[first * BS:stop, k * BS:(k + 1) * BS] = h
+        llo[first * BS:stop, k * BS:(k + 1) * BS] = l
+        return h, l
 
     def after(k):
-        hi, lo = split(w_ref[...] * srow[0:1, :])
-        whi[k], wlo[k] = hi, lo
-        if k + 1 == NB:
-            return
-        if k + 2 < NB:
-            for i, d in transfers(k + 2):
-                send_block(i, d)
-        todo = (transfers(0)[1:] if k == 0 else []) + transfers(k + 1)
-        for i, d in todo:
-            pass_block(i, d)
-        for i, d in todo:
-            take_block(i, d)
+        whi[k], wlo[k] = split(w_ref[...] * srow[0:1, :])
         if k == 0:
-            a_ref[BS:, :] = column(0)[BS:]
-        h, l = split(mm3(split(a_ref[BS:M - k * BS, :]), (hi, lo), True))
-        lhi[(k + 1) * BS:, k * BS:(k + 1) * BS] = h
-        llo[(k + 1) * BS:, k * BS:(k + 1) * BS] = l
-        a_ref[0:M - (k + 1) * BS, :] = column(k + 1)
+            low = panel(0, 1, ub[1].reshape(BS, BS))
+            a_ref[:BS, :] = ub[2].reshape(BS, BS) - mm3(low, low, True)
+            grams.hop(2)
+        elif k == 1:
+            grams.hop(3)
+            for d in (0, -1, -2, -3, 1, 2, 3):
+                grams.across(d)
+            grams.last()
+            grams.across(4)
+            panel(0, 2, column(0, 2))
+            panel(1, 2, column(1, 1))
+            a_ref[0:M - 2 * BS, :] = column(2)
+        elif k + 1 < NB:
+            panel(k, k + 1, a_ref[BS:M - k * BS, :])
+            a_ref[0:M - (k + 1) * BS, :] = column(k + 1)
 
     def step(k, _):
         diag_factor(a_ref, w_ref, srow)
@@ -326,6 +372,8 @@
             def _():
                 after(kk)
         return 0
+    a_ref[:BS, :] = ub[0].reshape(BS, BS)
+    grams.hop(1)
     lax.fori_loop(0, NB, step, 0)
 
     sel = lax.broadcasted_iota(jnp.int32, (64, M), 0) + v * 64 == lax.broadcasted_iota(jnp.int32, (64, M), 1)
@@ -337,12 +385,13 @@
         xhi[:, k * BS:(k + 1) * BS] = x[0]
         xlo[:, k * BS:(k + 1) * BS] = x[1]
     for d in (1, 2, 3):
-        for h in range(2):
-            arrive(other(d), 11 + d, h)
+        vectors.across(d)
     o_ref[...] = mm3((xhi[...], xlo[...]), split(gath[...].reshape(M, W)))
 
     for k in waits:
         k.wait_send()
+    vectors.finish()
+    grams.finish()
     for q in range(NQ):
         @pl.when(r != device_of(q))
         def _():
@@ -355,19 +404,19 @@
             return 0
         lax.fori_loop(1, NR, done, 0)
 
-    def sent(n, _):
-        rcopy(piece(0, 0, c), piece(0, 0, c), ts.at[n], tr.at[0], (r, sib)).wait_send()
-        return 0
-    lax.fori_loop(0, 32, sent, 0)
-
-    @pl.when(y >= 4)
-    def _():
-        lax.fori_loop(32, 40, sent, 0)
-    for k in range(NB):
-        for i, d in transfers(k):
-            @pl.when(y != i)
-            def _():
-                rcopy(piece(i, d, c), piece(i, d, c), tf.at[5 * i + d], tb.at[5 * i + d], (r, sib)).wait_send()
+    for n in range(3):
+        i, src, dst = early(n)
+
+        @pl.when(y == i)
+        def _():
+            def sent(m, _):
+                rcopy(src, dst, us.at[8 * n + m], ur.at[n], (r, sib)).wait_send()
+                return 0
+            lax.fori_loop(0, NY, sent, 0)
+
+        @pl.when(y != i)
+        def _():
+            rcopy(dst, dst, uf.at[n], ub_sem.at[n], (r, sib)).wait_send()
 
 
 def solve(tiles, columns, start, n_root=128.0):
@@ -376,21 +425,23 @@
     return pl.pallas_call(
         functools.partial(kernel, n_root),
         out_shape=jax.ShapeDtypeStruct((64, W), f32),
-        in_specs=[pl.BlockSpec(memory_space=pltpu.SMEM), vm, vm],
+        in_specs=[pl.BlockSpec(memory_space=pltpu.SMEM), pl.BlockSpec(memory_space=pl.ANY), pl.BlockSpec(memory_space=pl.ANY)],
         out_specs=vm,
         scratch_shapes=[
+            pltpu.VMEM((4, 6, BS, BS), bf16), pltpu.VMEM((64, W), f32),
             pltpu.VMEM((W, W + 2 * HALO), bf16), pltpu.VMEM((3, 64, W), f32),
             pltpu.VMEM((4, 64, HALO), f32), pltpu.VMEM((4, 64, HALO), f32),
             pltpu.VMEM((16, 64, W), f32), pltpu.VMEM((16, NQ, 16, BS), f32),
+            pltpu.VMEM((3, 2, 4, 16, BS), f32),
             pltpu.VMEM((NQ, 16, BS), f32), pltpu.VMEM((NR, 16, BS), f32),
             pltpu.VMEM((M, BS), f32), pltpu.VMEM((BS, BS), f32), pltpu.VMEM((8, BS), f32),
             pltpu.VMEM((NB, BS, BS), bf16), pltpu.VMEM((NB, BS, BS), bf16),
             pltpu.VMEM((M, M), bf16), pltpu.VMEM((M, M), bf16),
             pltpu.VMEM((64, M), f32), pltpu.VMEM((64, M), bf16), pltpu.VMEM((64, M), bf16),
-            dma((16,)), dma((8,)), dma((8,)), dma((32,)), dma((32,)),
+            dma((2,)), dma((16,)), dma((8,)), dma((8,)), dma((32,)), dma((32,)), dma((32,)), dma((32,)),
             dma((NQ,)), dma((NR,)), dma((NR,)), dma((NQ,)),
-            dma((40,)), dma((40,)), dma((40,)), dma((40,))],
-        compiler_params=pltpu.CompilerParams(collective_id=0, has_side_effects=True, vmem_limit_bytes=48 << 20),
+            dma((24,)), dma((3,)), dma((3,)), dma((3,))],
+        compiler_params=pltpu.CompilerParams(collective_id=0, has_side_effects=True, vmem_limit_bytes=56 << 20),
     )(columns, tiles, start)
 
 

time: 142 us -> 122 us (0.86)
  the two profiles are of different devices: /device:TPU:18 before, /device:TPU:1 now
where the time goes in v4:
time: 122 us
  Pallas kernels  120 us (98%)
  local copies, waits for them, and re-layouts  1.57 us (1%)
    pallas_call x1, Pallas kernels, solve(): pl.pallas_call(functools.partial(kernel, n_root), out_shape=jax.ShapeDtyp...  120 us

profile of v4, /device:TPU:1, one launch (start us, length us, event | category | flops | bytes accessed | tf_op | source)
XLA Modules:
  0.0 121.7 jit_solution(1496185459554974018)
XLA Ops:
  0.0 120.1 %shard_map.37 = f32[64,512]{1,0:T(8,128)} custom-call(s32[4,6]{1,0:T(4,128)} %columns_ref.1, bf16[4,6,128,128]{3,2,1,0:T(8,128)(2,1)} %tiles_in.1, f32[64,512]{1,0:T(8,128)} %y0_in.1), custom_call_target="tpu_custom_call" | custom-call | tf_op jit(solution)/shard_map/pallas_call | solution.py:425
  120.1 1.6 %copy.5 = f32[64,512]{1,0:T(8,128)} copy(f32[64,512]{1,0:T(8,128)} %shard_map.37) | data formatting | bytes 262144

commit v5 on v4

--- a/solution.py
+++ b/solution.py
@@ -89,10 +89,10 @@
     return (q * 8) // 5
 
 
-EARLY = ((0, 0), (1, 0), (1, 1))
-
-
-def kernel(n_root, columns_ref, tiles_in, y0_in, o_ref, tiles_ref, y0_ref, wt, ys, hl, hr, gath, gb, ub, part, inbox,
+EARLY = 3
+
+
+def kernel(n_root, columns_ref, tiles_in, y0_in, o_ref, tiles_ref, y0_ref, wt, ys, hl, hr, gath, gb, ub0, ub1, ub2, part, inbox,
            a_ref, w_ref, srow, whi, wlo, lhi, llo, r_ref, xhi, xlo,
            ls, hs, hrl, hrr, fs, fr, gs, gr, ds, dr, es, er, us, ur, uf, ub_sem):
     loads = [pltpu.make_async_copy(a, b, ls.at[n]) for n, (a, b) in enumerate(((y0_in, y0_ref), (tiles_in, tiles_ref)))]
@@ -283,45 +283,60 @@
     share(0)
     vectors.across(-3)
     gram_part(3)
+    share(1)
     vectors.last()
     vectors.across(4)
     gram_part(4)
-    for d in range(1, ND):
-        share(d)
-    shared(0)
-    shared(1)
-
-    def early(n):
-        i, j = EARLY[n]
-        d = i - j
-        return i, gb.at[v, 4 * d:4 * d + 4], ub.at[n, c]
-
-    for n in range(3):
-        i, src, dst = early(n)
+
+    ub = (ub0, ub1, ub2)
+
+    def early(i, core):
+        return gb.at[v, :4 * i + 4], ub[i].at[core]
+
+    def send_early(i):
+        src, dst = early(i, c)
 
         @pl.when(y == i)
         def _():
-            ub[n, c] = src[...]
-            rcopy(src, dst, us.at[8 * n], ub_sem.at[n], (r, sib)).start()
+            dst[...] = src[...]
+            rcopy(src, dst, us.at[8 * i], ub_sem.at[i], (r, sib)).start()
 
             def one(m, _):
-                rcopy(src, dst, us.at[8 * n + m], ur.at[n], (r, lax.rem(y + m, NY) * 2 + c)).start()
+                rcopy(src, dst, us.at[8 * i + m], ur.at[i], (r, lax.rem(y + m, NY) * 2 + c)).start()
                 return 0
             lax.fori_loop(1, NY, one, 0)
+
+    def pass_early(i):
+        dst = early(i, c)[1]
+
+        @pl.when(y != i)
+        def _():
+            rcopy(dst, dst, us.at[0], ur.at[i], (r, sib)).wait_recv()
+            rcopy(dst, dst, uf.at[i], ub_sem.at[i], (r, sib)).start()
+
+    def take_early(i):
+        dst = early(i, 1 - c)[1]
+        rcopy(dst, dst, us.at[0], ub_sem.at[i], (r, sib)).wait_recv()
+
+    shared(0)
+    send_early(0)
+    shared(1)
+    send_early(1)
     for d in range(2, ND):
-        shared(d)
+        share(d)
+    shared(2)
+    send_early(2)
+    pass_early(0)
+    pass_early(1)
+    shared(3)
+    shared(4)
     for h in range(2):
         grams.first(h)
-    for n in range(3):
-        i, src, dst = early(n)
-
-        @pl.when(y != i)
-        def _():
-            rcopy(dst, dst, us.at[0], ur.at[n], (r, sib)).wait_recv()
-            rcopy(dst, dst, uf.at[n], ub_sem.at[n], (r, sib)).start()
-    for n in range(3):
-        dst = ub.at[n, 1 - c]
-        rcopy(dst, dst, us.at[0], ub_sem.at[n], (r, sib)).wait_recv()
+    take_early(0)
+    take_early(1)
+
+    def ahead(i, j):
+        return ub[i][:, 4 * (i - j):4 * (i - j) + 4].reshape(BS, BS)
 
     def block(i, j):
         d = i - j
@@ -349,18 +364,26 @@
     def after(k):
         whi[k], wlo[k] = split(w_ref[...] * srow[0:1, :])
         if k == 0:
-            low = panel(0, 1, ub[1].reshape(BS, BS))
-            a_ref[:BS, :] = ub[2].reshape(BS, BS) - mm3(low, low, True)
+            grams.hop(1)
+            low = panel(0, 1, ahead(1, 0))
+            a_ref[:BS, :] = ahead(1, 1) - mm3(low, low, True)
+            pass_early(2)
+        elif k == 1:
+            take_early(2)
             grams.hop(2)
-        elif k == 1:
+            low = panel(0, 2, ahead(2, 0))
+            above = (lhi[BS:2 * BS, :BS], llo[BS:2 * BS, :BS])
+            next_low = panel(1, 2, ahead(2, 1) - mm3(low, above, True))
+            a_ref[:BS, :] = ahead(2, 2) - mm3(low, low, True) - mm3(next_low, next_low, True)
+        elif k == 2:
             grams.hop(3)
             for d in (0, -1, -2, -3, 1, 2, 3):
                 grams.across(d)
             grams.last()
             grams.across(4)
-            panel(0, 2, column(0, 2))
-            panel(1, 2, column(1, 1))
-            a_ref[0:M - 2 * BS, :] = column(2)
+            for j in range(EARLY):
+                panel(j, EARLY, column(j, EARLY - j))
+            a_ref[0:M - EARLY * BS, :] = column(EARLY)
         elif k + 1 < NB:
             panel(k, k + 1, a_ref[BS:M - k * BS, :])
             a_ref[0:M - (k + 1) * BS, :] = column(k + 1)
@@ -372,8 +395,7 @@
             def _():
                 after(kk)
         return 0
-    a_ref[:BS, :] = ub[0].reshape(BS, BS)
-    grams.hop(1)
+    a_ref[:BS, :] = ahead(0, 0)
     lax.fori_loop(0, NB, step, 0)
 
     sel = lax.broadcasted_iota(jnp.int32, (64, M), 0) + v * 64 == lax.broadcasted_iota(jnp.int32, (64, M), 1)
@@ -404,19 +426,19 @@
             return 0
         lax.fori_loop(1, NR, done, 0)
 
-    for n in range(3):
-        i, src, dst = early(n)
+    for i in range(EARLY):
+        src, dst = early(i, c)
 
         @pl.when(y == i)
         def _():
             def sent(m, _):
-                rcopy(src, dst, us.at[8 * n + m], ur.at[n], (r, sib)).wait_send()
+                rcopy(src, dst, us.at[8 * i + m], ur.at[i], (r, sib)).wait_send()
                 return 0
             lax.fori_loop(0, NY, sent, 0)
 
         @pl.when(y != i)
         def _():
-            rcopy(dst, dst, uf.at[n], ub_sem.at[n], (r, sib)).wait_send()
+            rcopy(dst, dst, uf.at[i], ub_sem.at[i], (r, sib)).wait_send()
 
 
 def solve(tiles, columns, start, n_root=128.0):
@@ -432,7 +454,7 @@
             pltpu.VMEM((W, W + 2 * HALO), bf16), pltpu.VMEM((3, 64, W), f32),
             pltpu.VMEM((4, 64, HALO), f32), pltpu.VMEM((4, 64, HALO), f32),
             pltpu.VMEM((16, 64, W), f32), pltpu.VMEM((16, NQ, 16, BS), f32),
-            pltpu.VMEM((3, 2, 4, 16, BS), f32),
+            pltpu.VMEM((2, 4, 16, BS), f32), pltpu.VMEM((2, 8, 16, BS), f32), pltpu.VMEM((2, 12, 16, BS), f32),
             pltpu.VMEM((NQ, 16, BS), f32), pltpu.VMEM((NR, 16, BS), f32),
             pltpu.VMEM((M, BS), f32), pltpu.VMEM((BS, BS), f32), pltpu.VMEM((8, BS), f32),
             pltpu.VMEM((NB, BS, BS), bf16), pltpu.VMEM((NB, BS, BS), bf16),

time: 122 us -> 120 us (0.984)
  Pallas kernels: 120 us -> 117 us
    pallas_call x1, Pallas kernels: 120 us -> 117 us  [solve(): pl.pallas_call(functools.partial(kernel, n_root), out_shape=jax.ShapeDtyp...]
where the time goes in v5:
time: 120 us; the launch traced here: 119 us
  Pallas kernels  117 us (98%)
  local copies, waits for them, and re-layouts  1.57 us (1%)
    pallas_call x1, Pallas kernels, solve(): pl.pallas_call(functools.partial(kernel, n_root), out_shape=jax.ShapeDtyp...  117 us

profile of v5, /device:TPU:1, one launch (start us, length us, event | category | flops | bytes accessed | tf_op | source)
XLA Modules:
  0.0 119.0 jit_solution(2006026017313373824)
XLA Ops:
  0.0 117.4 %shard_map.37 = f32[64,512]{1,0:T(8,128)} custom-call(s32[4,6]{1,0:T(4,128)} %columns_ref.1, bf16[4,6,128,128]{3,2,1,0:T(8,128)(2,1)} %tiles_in.1, f32[64,512]{1,0:T(8,128)} %y0_in.1), custom_call_target="tpu_custom_call" | custom-call | tf_op jit(solution)/shard_map/pallas_call | solution.py:447
  117.4 1.6 %copy.5 = f32[64,512]{1,0:T(8,128)} copy(f32[64,512]{1,0:T(8,128)} %shard_map.37) | data formatting | bytes 262144

commit v6 on v5

--- a/solution.py
+++ b/solution.py
@@ -169,16 +169,32 @@
         def other(d):
             return lax.rem(y + NY + d, NY) * 2 + 1 - c
 
+        def each(i, h, act):
+            for when, ref in half(i, h):
+                if when is None:
+                    act(ref)
+                else:
+                    @pl.when(when)
+                    def _():
+                        act(ref)
+
         def go(i, n, h, to):
-            rcopy(half(i, h), half(i, h), send.at[2 * n + h], recv.at[2 * n + h], (r, to)).start()
+            each(i, h, lambda ref: rcopy(ref, ref, send.at[2 * n + h], recv.at[2 * n + h], (r, to)).start())
             started.add((n, h))
+
+        def arrive(i, n, h):
+            each(i, h, lambda ref: rcopy(ref, ref, send.at[2 * n + h], recv.at[2 * n + h], (r, sib)).wait_recv())
+
+        def origin(n):
+            if n < 4:
+                return slot(-n)
+            if n < 8:
+                return slot(n - 4)
+            return slot(n - 11) if n < 15 else slot(4)
 
         def finish():
             for n, h in sorted(started):
-                rcopy(half(v, h), half(v, h), send.at[2 * n + h], recv.at[2 * n + h], (r, sib)).wait_send()
-
-        def arrive(i, n, h):
-            rcopy(half(i, h), half(i, h), send.at[2 * n + h], recv.at[2 * n + h], (r, sib)).wait_recv()
+                each(origin(n), h, lambda ref: rcopy(ref, ref, send.at[2 * n + h], recv.at[2 * n + h], (r, sib)).wait_send())
 
         def first(h):
             go(v, 0, h, yr)
@@ -207,8 +223,11 @@
             go(slot(4), 15, 1, sib)
         return types.SimpleNamespace(first=first, hop=hop, across=across, last=last, finish=finish)
 
-    vectors = ring(lambda i, h: gath.at[i, rows_of[h]], fs, fr)
-    grams = ring(lambda i, h: gb.at[i, 10 * h:10 * h + 10], gs, gr)
+    def gram_half(i, h):
+        return ((i < 2 * EARLY, gb.at[i, 4 + 6 * h:10 + 6 * h]), (i >= 2 * EARLY, gb.at[i, 10 * h:10 * h + 10]))
+
+    vectors = ring(lambda i, h: ((None, gath.at[i, rows_of[h]]),), fs, fr)
+    grams = ring(gram_half, gs, gr)
 
     halo(0, 0, True)
     halo(0, 1, True)
@@ -326,12 +345,12 @@
         share(d)
     shared(2)
     send_early(2)
+    grams.first(0)
     pass_early(0)
     pass_early(1)
     shared(3)
     shared(4)
-    for h in range(2):
-        grams.first(h)
+    grams.first(1)
     take_early(0)
     take_early(1)
 

time: 120 us -> 118 us (0.983)
  no operation moved by 1% of the time
where the time goes in v6:
time: 118 us
  Pallas kernels  116 us (98%)
  local copies, waits for them, and re-layouts  1.57 us (1%)
    pallas_call x1, Pallas kernels, solve(): pl.pallas_call(functools.partial(kernel, n_root), out_shape=jax.ShapeDtyp...  116 us

profile of v6, /device:TPU:1, one launch (start us, length us, event | category | flops | bytes accessed | tf_op | source)
XLA Modules:
  0.0 117.9 jit_solution(14038945469156105077)
XLA Ops:
  0.0 116.3 %shard_map.37 = f32[64,512]{1,0:T(8,128)} custom-call(s32[4,6]{1,0:T(4,128)} %columns_ref.1, bf16[4,6,128,128]{3,2,1,0:T(8,128)(2,1)} %tiles_in.1, f32[64,512]{1,0:T(8,128)} %y0_in.1), custom_call_target="tpu_custom_call" | custom-call | tf_op jit(solution)/shard_map/pallas_call | solution.py:466
  116.3 1.6 %copy.5 = f32[64,512]{1,0:T(8,128)} copy(f32[64,512]{1,0:T(8,128)} %shard_map.37) | data formatting | bytes 262144

commit v7 on v6

--- a/solution.py
+++ b/solution.py
@@ -150,8 +150,8 @@
 
     def halo(s, h, go):
         src, n = field(s), 2 * s + h
-        to_right = rcopy(src.at[rows_of[h], W - HALO:], hl.at[s, rows_of[h]], hs.at[2 * n], hrl.at[n], (right, v))
-        to_left = rcopy(src.at[rows_of[h], :HALO], hr.at[s, rows_of[h]], hs.at[2 * n + 1], hrr.at[n], (left, v))
+        to_right = rcopy(src.at[:, W - HALO:], hl.at[s], hs.at[2 * n], hrl.at[n], (right, v))
+        to_left = rcopy(src.at[:, :HALO], hr.at[s], hs.at[2 * n + 1], hrr.at[n], (left, v))
         if go:
             to_right.start()
             to_left.start()
@@ -230,11 +230,10 @@
     grams = ring(gram_half, gs, gr)
 
     halo(0, 0, True)
-    halo(0, 1, True)
     for s in range(4):
         acc = halves(mm(stacked(field(s)[...]), wt[:, HALO:HALO + W], True))
-        for h in range(2):
-            rows = rows_of[h]
+        for h in range(1):
+            rows = slice(0, 64)
             halo(s, h, False)
             wl = halves(mm(stacked(hl[s, rows]), wt[:HALO, :HALO], True))
             wr = halves(mm(stacked(hr[s, rows]), wt[BS:, HALO + W:], True))
@@ -248,7 +247,8 @@
                 halo(s + 1, h, True)
             else:
                 gath[v, rows] = new
-                vectors.first(h)
+                vectors.first(0)
+                vectors.first(1)
 
     own = split(gath[v])
 

time: 118 us -> 121 us (1.025)
  Pallas kernels: 116 us -> 119 us
    pallas_call x1, Pallas kernels: 116 us -> 119 us  [solve(): pl.pallas_call(functools.partial(kernel, n_root), out_shape=jax.ShapeDtyp...]
where the time goes in v7:
time: 121 us
  Pallas kernels  119 us (98%)
  local copies, waits for them, and re-layouts  1.57 us (1%)
    pallas_call x1, Pallas kernels, solve(): pl.pallas_call(functools.partial(kernel, n_root), out_shape=jax.ShapeDtyp...  119 us

profile of v7, /device:TPU:1, one launch (start us, length us, event | category | flops | bytes accessed | tf_op | source)
XLA Modules:
  0.0 120.8 jit_solution(12592946409361419445)
XLA Ops:
  0.0 119.2 %shard_map.37 = f32[64,512]{1,0:T(8,128)} custom-call(s32[4,6]{1,0:T(4,128)} %columns_ref.1, bf16[4,6,128,128]{3,2,1,0:T(8,128)(2,1)} %tiles_in.1, f32[64,512]{1,0:T(8,128)} %y0_in.1), custom_call_target="tpu_custom_call" | custom-call | tf_op jit(solution)/shard_map/pallas_call | solution.py:466
  119.2 1.6 %copy.5 = f32[64,512]{1,0:T(8,128)} copy(f32[64,512]{1,0:T(8,128)} %shard_map.37) | data formatting | bytes 262144
